TPU v7x, 128 devices: a whole 4x4x4 slice. The times are simulated.
128 devices in a mesh: dp: 8 (over x, core), expert: 16 (over y, z).
Axes of the slice: x: 4, y: 4, z: 4, core: 2. Of those that a mesh axis runs over, the one named last changes fastest.
Arguments:
- tokens: bfloat16 [20480, 4096], P(('dp', 'expert')), may hold values from -6 to 6
- gate_probs: float32 [20480, 2], P(('dp', 'expert')), may hold values from 0.2 to 1
- expert_ids: int32 [20480, 2], P(('dp', 'expert')), may hold values from 0 to 15, all different within a row
- placement: int32 [16, 8], replicated, may hold values from 0 to 7, as said below
- replica: int32 [20480, 2], P(('dp', 'expert')), may hold values from 0 to 7
- row_counts: int32 [128], P(('dp', 'expert')), may hold values from 120 to 160
- w_gate: bfloat16 [16, 4096, 768], P('expert'), may hold values from -0.09375 to 0.09375
- w_up: bfloat16 [16, 4096, 768], P('expert'), may hold values from -0.09375 to 0.09375
- w_down: bfloat16 [16, 768, 4096], P('expert'), may hold values from -0.21875 to 0.21875
- d_out: bfloat16 [20480, 4096], P(('dp', 'expert')), may hold values from -6 to 6
Outputs:
- layer_out: bfloat16 [20480, 4096], P(('dp', 'expert'))
- d_tokens: bfloat16 [20480, 4096], P(('dp', 'expert'))
- d_gates: float32 [20480, 2], P(('dp', 'expert'))
- g_gate: bfloat16 [16, 4096, 768], P('expert', 'dp')
- g_up: bfloat16 [16, 4096, 768], P('expert', 'dp')
- g_down: bfloat16 [16, 768, 4096], P('expert', None, 'dp')
Inputs may be any that keep to these rules, and one draw needn't show every extreme that they name: `placement`: each expert's list names 1 to 8 distinct dp indices, repeated in order; in every draw some expert's list names all of them.
All inputs are finite; a program needn't handle non-finite values.
Results may differ from a plain program's by a relative error of at most 0.015.
Values may be sent and summed in bfloat16 or wider, within the bound.
A program may use at most 192 MiB of HBM per device.

v0:
```python
import jax
import jax.numpy as jnp
from jax import lax
from jax.sharding import PartitionSpec as P


def silu_parts(gate_pre):
    sigma = jax.nn.sigmoid(gate_pre)
    return (gate_pre * sigma, sigma * (1.0 + gate_pre * (1.0 - sigma)))


def move_rows(payload):
    return lax.all_to_all(payload, ("dp", "expert"), split_axis=0, concat_axis=0, tiled=True)


def forward_rows(rows_x, gate_mat, up_mat, down_mat):
    pre_g = jnp.dot(rows_x, gate_mat, preferred_element_type=jnp.float32)
    pre_u = jnp.dot(rows_x, up_mat, preferred_element_type=jnp.float32)
    silu_val, silu_slope = silu_parts(pre_g)
    hidden = (silu_val * pre_u).astype(jnp.bfloat16)
    expert_out = jnp.dot(hidden, down_mat, preferred_element_type=jnp.float32).astype(jnp.bfloat16)
    return (pre_u, silu_val, silu_slope, hidden, expert_out)


def backward_rows(rows_x, cotan, fwd_state, gate_mat, up_mat, down_mat):
    pre_u, silu_val, silu_slope, hidden, expert_out = fwd_state
    contract_last = (((1,), (1,)), ((), ()))
    contract_first = (((0,), (0,)), ((), ()))
    d_hidden = lax.dot_general(cotan, down_mat, contract_last, preferred_element_type=jnp.float32)
    d_pre_g = (d_hidden * pre_u * silu_slope).astype(jnp.bfloat16)
    d_pre_u = (d_hidden * silu_val).astype(jnp.bfloat16)
    pick_dx = (
        lax.dot_general(d_pre_g, gate_mat, contract_last, preferred_element_type=jnp.float32)
        + lax.dot_general(d_pre_u, up_mat, contract_last, preferred_element_type=jnp.float32)
    ).astype(jnp.bfloat16)
    part_g = lax.dot_general(rows_x, d_pre_g, contract_first, preferred_element_type=jnp.float32)
    part_u = lax.dot_general(rows_x, d_pre_u, contract_first, preferred_element_type=jnp.float32)
    part_d = lax.dot_general(cotan, hidden, contract_first, preferred_element_type=jnp.float32)
    return (pick_dx, jnp.stack([part_g, part_u, part_d]))


def on_device(
    tokens, gate_probs, expert_ids, placement, replica, row_counts, w_gate, w_up, w_down, d_out
):
    dp_size = lax.axis_size("dp")
    expert_size = lax.axis_size("expert")
    devices = dp_size * expert_size
    tok_dev, model_width = tokens.shape
    top_count = gate_probs.shape[1]
    pick_count = tok_dev * top_count
    capacity = max(2, 3 * pick_count // (4 * devices))
    slot_count = devices * capacity
    flat_ids = expert_ids.reshape(pick_count)
    flat_rep = replica.reshape(pick_count)
    pair_match = (flat_ids[:, None, None] == jnp.arange(expert_size)[None, :, None]) & (
        flat_rep[:, None, None] == jnp.arange(dp_size)[None, None, :]
    )
    dest_row = jnp.sum(jnp.where(pair_match, placement[None, :, :], 0), axis=(1, 2))
    target = dest_row * expert_size + flat_ids
    living = jnp.arange(pick_count) // top_count < row_counts[0]
    dest_hits = (target[:, None] == jnp.arange(devices)[None, :]) & living[:, None]
    prefix_count = jnp.cumsum(dest_hits.astype(jnp.int32), axis=0) - 1
    rank_of = jnp.sum(jnp.where(dest_hits, prefix_count, 0), axis=1)
    keeping = living & (rank_of < capacity)
    slot_place = jnp.where(keeping, target * capacity + rank_of, slot_count)
    slot_pick = (
        jnp.full((slot_count,), -1, jnp.int32)
        .at[slot_place]
        .set(jnp.arange(pick_count, dtype=jnp.int32), mode="drop")
    )
    filled = slot_pick >= 0
    safe_pick = jnp.where(filled, slot_pick, 0)
    token_idx = safe_pick // top_count
    weight = jnp.where(filled, gate_probs.reshape(pick_count)[safe_pick], 0.0)
    send_x = jnp.where(filled[:, None], tokens[token_idx], 0)
    raw_cot = d_out[token_idx].astype(jnp.float32)
    send_cot = (raw_cot * weight[:, None]).astype(jnp.bfloat16)
    gate_mat = w_gate[0]
    up_mat = w_up[0]
    down_mat = w_down[0]
    recv_x = move_rows(send_x.reshape(devices, capacity, model_width)).reshape(
        slot_count, model_width
    )
    fwd_state = forward_rows(recv_x, gate_mat, up_mat, down_mat)
    back_out = move_rows(fwd_state[4].reshape(devices, capacity, model_width)).reshape(
        slot_count, model_width
    )
    recv_cot = move_rows(send_cot.reshape(devices, capacity, model_width)).reshape(
        slot_count, model_width
    )
    pick_dx, partial_value = backward_rows(recv_x, recv_cot, fwd_state, gate_mat, up_mat, down_mat)
    back_dx = move_rows(pick_dx.reshape(devices, capacity, model_width)).reshape(
        slot_count, model_width
    )
    out_f = back_out.astype(jnp.float32)
    layer_out = (
        jnp.zeros((tok_dev, model_width), jnp.float32).at[token_idx].add(weight[:, None] * out_f)
    )
    d_tokens = (
        jnp.zeros((tok_dev, model_width), jnp.float32)
        .at[token_idx]
        .add(jnp.where(filled[:, None], back_dx.astype(jnp.float32), 0.0))
    )
    pick_grad = jnp.where(filled, jnp.sum(raw_cot * out_f, axis=1), 0.0)
    d_gates = (
        jnp.zeros((pick_count,), jnp.float32)
        .at[safe_pick]
        .add(pick_grad)
        .reshape(tok_dev, top_count)
    )
    summed = lax.psum_scatter(
        partial_value.astype(jnp.bfloat16), "dp", scatter_dimension=1, tiled=True
    ).astype(jnp.float32)
    g_gate = summed[0].astype(jnp.bfloat16)[None]
    g_up = summed[1].astype(jnp.bfloat16)[None]
    g_down = summed[2].T.astype(jnp.bfloat16)[None]
    return (
        layer_out.astype(jnp.bfloat16),
        d_tokens.astype(jnp.bfloat16),
        d_gates,
        g_gate,
        g_up,
        g_down,
    )


def solution(mesh):
    return jax.shard_map(
        on_device,
        mesh=mesh,
        in_specs=(
            P(("dp", "expert"), None),
            P(("dp", "expert"), None),
            P(("dp", "expert"), None),
            P(),
            P(("dp", "expert"), None),
            P(("dp", "expert")),
            P("expert", None, None),
            P("expert", None, None),
            P("expert", None, None),
            P(("dp", "expert"), None),
        ),
        out_specs=(
            P(("dp", "expert"), None),
            P(("dp", "expert"), None),
            P(("dp", "expert"), None),
            P("expert", "dp", None),
            P("expert", "dp", None),
            P("expert", None, "dp"),
        ),
        check_vma=False,
    )
```

profile of v0, /device:TPU:1, one launch (start us, length us, event | category | flops | bytes accessed | tf_op | source)
XLA Modules:
  0.0 320.1 jit_solution(16122084647812823170)
XLA Ops:
  19.3 3.5 %broadcast_select_fusion = bf16[128,2,4096]{2,1,0:T(2,128)(2,1)S(1)} fusion(bf16[128,2,4096]{2,1,0:T(2,128)(2,1)} %gather.13, pred[128,2]{1,0:T(8,128)(4,1)S(1)} %broadcast_in_dim.93), kind=kLoop, calls=%fused_computation.35 | loop fusion | flops 1048576 | bytes 4194560 | tf_op jit(solution)/shard_map/jit(_where)/select_n | solution.py:75
  22.7 41.4 %all_to_all.20 = bf16[128,2,4096]{2,1,0:T(2,128)(2,1)} all-to-all(bf16[128,2,4096]{2,1,0:T(2,128)(2,1)S(1)} %broadcast_select_fusion), channel_id=1, replica_groups=mesh['dp'=8,'expert'=16] {'dp','expert'}, dimensions={0} | all-to-all | bytes 4194304 | tf_op jit(solution)/shard_map/all_to_all | solution.py:13
  66.9 4.6 %fusion.10 = f32[256,768]{1,0:T(8,128)S(1)} fusion(bf16[256,4096]{1,0:T(8,128)(2,1)S(1)} %reshape.218, bf16[1,4096,768]{2,1,0:T(8,128)(2,1)} %param.16), kind=kOutput, calls=%fused_computation.21 | convolution fusion | flops 1610612736 | bytes 9175040 | tf_op jit(solution)/shard_map/dot_general | solution.py:17
  71.5 5.7 %multiply_convert_fusion.3 = (bf16[256,768]{1,0:T(8,128)(2,1)S(1)}, f32[256,768]{1,0:T(8,128)}) fusion(f32[256,768]{1,0:T(8,128)S(1)} %fusion.10, bf16[256,4096]{1,0:T(8,128)(2,1)S(1)} %reshape.218, bf16[1,4096,768]{2,1,0:T(8,128)(2,1)} %param.17), kind=kOutput, calls=%fused_computation.44 | convolution fusion | flops 1611792384 | bytes 10354688 | tf_op jit(solution)/shard_map/dot_general | solution.py:18
  78.0 5.9 %fusion.21 = bf16[256,4096]{1,0:T(8,128)(2,1)} fusion(bf16[256,768]{1,0:T(8,128)(2,1)S(1)} %get-tuple-element.35, bf16[1,768,4096]{2,1,0:T(8,128)(2,1)} %param.18), kind=kOutput, calls=%fused_computation.28 | convolution fusion | flops 1611661312 | bytes 8781824 | tf_op jit(solution)/shard_map/dot_general | solution.py:21
  83.9 4.5 %reshape.219 = bf16[128,2,4096]{2,1,0:T(2,128)(2,1)} reshape(bf16[256,4096]{1,0:T(8,128)(2,1)} %fusion.21) | data formatting | bytes 4194304 | tf_op jit(solution)/shard_map/reshape | solution.py:85
  88.4 5.8 %all-to-all-start.1 = ((bf16[128,2,4096]{2,1,0:T(2,128)(2,1)}), bf16[128,2,4096]{2,1,0:T(2,128)(2,1)}, u32[]{:S(2)}, u32[]{:S(2)}) async-start(bf16[128,2,4096]{2,1,0:T(2,128)(2,1)} %reshape.219), calls=%async_computation.1 | async-start | bytes 4194304 | tf_op jit(solution)/shard_map/all_to_all | solution.py:13
  96.7 3.2 gather_fusion.2
  99.9 5.4 %reshape.225 = f32[128,2,4096]{2,1,0:T(2,128)} reshape(bf16[256,4096]{1,0:T(8,128)(2,1)} %gather_fusion.2) | data formatting | bytes 6291456 | tf_op jit(solution)/shard_map/convert_element_type | solution.py:76
  105.3 18.2 %all-to-all-done.1 = bf16[128,2,4096]{2,1,0:T(2,128)(2,1)} async-done(((bf16[128,2,4096]{2,1,0:T(2,128)(2,1)}), bf16[128,2,4096]{2,1,0:T(2,128)(2,1)}, u32[]{:S(2)}, u32[]{:S(2)}) %all-to-all-start.1) | async-done | bytes 2097184 | tf_op jit(solution)/shard_map/all_to_all | solution.py:13
  123.5 6.0 %multiply_reduce_fusion = (f32[128,2]{1,0:T(8,128)S(1)}, bf16[128,2,4096]{2,1,0:T(2,128)(2,1)S(1)}) fusion(f32[128,2,4096]{2,1,0:T(2,128)} %reshape.225, bf16[128,2,4096]{2,1,0:T(2,128)(2,1)} %all-to-all-done.1, f32[128,2]{1,0:T(8,128)S(1)} %mul.81), kind=kLoop, calls=%fused_computation.29 | loop fusion | flops 5242624 | bytes 8390656 | tf_op jit(solution)/shard_map/reduce_sum | solution.py:104
  129.5 34.7 %all_to_all.21 = bf16[128,2,4096]{2,1,0:T(2,128)(2,1)} all-to-all(bf16[128,2,4096]{2,1,0:T(2,128)(2,1)S(1)} %get-tuple-element.25), channel_id=1, replica_groups=mesh['dp'=8,'expert'=16] {'dp','expert'}, dimensions={0} | all-to-all | bytes 4194304 | tf_op jit(solution)/shard_map/all_to_all | solution.py:13
  164.2 4.1 %reshape.220 = bf16[256,4096]{1,0:T(8,128)(2,1)} reshape(bf16[128,2,4096]{2,1,0:T(2,128)(2,1)} %all_to_all.21) | data formatting | bytes 4194304 | tf_op jit(solution)/shard_map/reshape | solution.py:88
  168.3 3.6 %fusion.14 = bf16[1,4096,768]{2,1,0:T(8,128)(2,1)S(1)} fusion(bf16[256,4096]{1,0:T(8,128)(2,1)} %reshape.220, bf16[256,768]{1,0:T(8,128)(2,1)S(1)} %copy-done.5), kind=kOutput, calls=%fused_computation.25 | convolution fusion | flops 1613758464 | bytes 8781824 | tf_op jit(solution)/shard_map/dot_general | solution.py:38
  171.9 4.8 %multiply_convert_fusion.2 = (bf16[256,768]{1,0:T(8,128)(2,1)S(1)}, bf16[256,768]{1,0:T(8,128)(2,1)S(1)}) fusion(f32[256,768]{1,0:T(8,128)S(1)} %copy-done.8, f32[256,768]{1,0:T(8,128)S(1)} %copy-done.9, bf16[256,4096]{1,0:T(8,128)(2,1)S(1)} %copy-done.3, bf16[1,768,4096]{2,1,0:T(8,128)(2,1)} %param.18), kind=kOutput, calls=%fused_computation.43 | convolution fusion | flops 1613168640 | bytes 10747904 | tf_op jit(solution)/shard_map/dot_general | solution.py:29
  180.5 8.1 %pad_maximum_fusion = bf16[3,4096,768]{2,1,0:T(8,128)(2,1)} fusion(bf16[1,4096,768]{2,1,0:T(8,128)(2,1)S(1)} %fusion.14, bf16[1,4096,768]{2,1,0:T(8,128)(2,1)S(1)} %fusion.13, bf16[1,4096,768]{2,1,0:T(8,128)(2,1)S(1)} %fusion.12), kind=kLoop, calls=%fused_computation.7 | loop fusion | flops 18874368 | bytes 37748736 | tf_op jit(solution)/shard_map/stack | solution.py:39
  188.6 4.6 %fusion.4 = f32[256,4096]{1,0:T(8,128)S(1)} fusion(bf16[256,768]{1,0:T(8,128)(2,1)S(1)} %get-tuple-element.30, bf16[1,4096,768]{2,1,0:T(8,128)(2,1)} %param.17), kind=kOutput, calls=%fused_computation.15 | convolution fusion | flops 1610612736 | bytes 10878976 | tf_op jit(solution)/shard_map/dot_general | solution.py:34
  193.2 5.5 %fusion.18 = bf16[256,4096]{1,0:T(8,128)(2,1)S(1)} fusion(f32[256,4096]{1,0:T(8,128)S(1)} %fusion.4, bf16[256,768]{1,0:T(8,128)(2,1)S(1)} %get-tuple-element.29, bf16[1,4096,768]{2,1,0:T(8,128)(2,1)} %param.16), kind=kOutput, calls=%fused_computation.27 | convolution fusion | flops 1612709888 | bytes 12976128 | tf_op jit(solution)/shard_map/dot_general | solution.py:33
  201.4 4.6 %all-to-all-start.3 = ((bf16[128,2,4096]{2,1,0:T(2,128)(2,1)}), bf16[128,2,4096]{2,1,0:T(2,128)(2,1)S(1)}, u32[]{:S(2)}, u32[]{:S(2)}) async-start(bf16[128,2,4096]{2,1,0:T(2,128)(2,1)} %reshape.221), calls=%async_computation.3 | async-start | bytes 4194304 | tf_op jit(solution)/shard_map/all_to_all | solution.py:13
  209.2 4.4 %reshape.224 = f32[256,4096]{1,0:T(8,128)} reshape(bf16[128,2,4096]{2,1,0:T(2,128)(2,1)} %all-to-all-done.1) | data formatting | bytes 6291456 | tf_op jit(solution)/shard_map/convert_element_type | solution.py:95
  213.7 9.7 %scatter_custom_fusion.1 = f32[160,4096]{1,0:T(8,128)} fusion(s32[256]{0:T(256)S(1)} %get-tuple-element.34, f32[256,4096]{1,0:T(8,128)} %reshape.224, f32[256]{0:T(256)S(1)} %broadcast_select_fusion.2, f32[]{:T(128)} %constant.45.clone.1), kind=kCustom, calls=%fused_computation.33 | custom fusion | flops 2097152 | bytes 6816772 | tf_op jit(solution)/shard_map/scatter-add | solution.py:97
  226.4 19.6 %all-to-all-done.3 = bf16[128,2,4096]{2,1,0:T(2,128)(2,1)S(1)} async-done(((bf16[128,2,4096]{2,1,0:T(2,128)(2,1)}), bf16[128,2,4096]{2,1,0:T(2,128)(2,1)S(1)}, u32[]{:S(2)}, u32[]{:S(2)}) %all-to-all-start.3) | async-done | bytes 2097184 | tf_op jit(solution)/shard_map/all_to_all | solution.py:13
  248.6 9.7 %scatter_custom_fusion.2 = f32[160,4096]{1,0:T(8,128)} fusion(s32[256]{0:T(256)S(1)} %get-tuple-element.34, f32[256,4096]{1,0:T(8,128)} %reshape.226, f32[]{:T(128)} %constant.45.clone.1, pred[256]{0:T(512)(128)(4,1)S(1)} %broadcast_compare_fusion), kind=kCustom, calls=%fused_computation.30 | custom fusion | flops 2097152 | bytes 6817280 | tf_op jit(solution)/shard_map/scatter-add | solution.py:102
  261.4 47.6 %reduce-scatter.2.cloned.1.call-done = bf16[3,512,768]{2,1,0:T(8,128)(2,1)} async-done(((bf16[3,4096,768]{2,1,0:T(8,128)(2,1)}), bf16[3,512,768]{2,1,0:T(8,128)(2,1)}) %reduce-scatter.2.cloned.1.call-update) | async-done | bytes 2359312 | tf_op jit(solution)/shard_map/reduce_scatter | solution.py:111
  (69 shorter events, 39.6 us)
Async XLA Ops:
  7.2 7.6 %copy-start = (bf16[160,4096]{1,0:T(8,128)(2,1)S(1)}, bf16[160,4096]{1,0:T(8,128)(2,1)}, u32[]{:S(2)}) copy-start(bf16[160,4096]{1,0:T(8,128)(2,1)} %param.10) | copy-start | bytes 3932164
  71.5 5.8 %copy-start.7 = (f32[256,768]{1,0:T(8,128)}, f32[256,768]{1,0:T(8,128)S(1)}, u32[]{:S(2)}) copy-start(f32[256,768]{1,0:T(8,128)S(1)} %fusion.10) | copy-start | bytes 2359300
  77.2 0.7 copy-start.4
  83.9 10.3 %copy-start.6 = (f32[160,2]{0,1:T(2,128)S(1)}, f32[160,2]{0,1:T(2,128)}, u32[]{:S(2)}) copy-start(f32[160,2]{0,1:T(2,128)} %param.11) | copy-start | bytes 3844
  83.9 12.7 %copy-start.2 = (bf16[160,4096]{1,0:T(8,128)(2,1)S(1)}, bf16[160,4096]{1,0:T(8,128)(2,1)}, u32[]{:S(2)}) copy-start(bf16[160,4096]{1,0:T(8,128)(2,1)} %param.19) | copy-start | bytes 3932164
  88.4 35.1 %all-to-all-start.1 = ((bf16[128,2,4096]{2,1,0:T(2,128)(2,1)}), bf16[128,2,4096]{2,1,0:T(2,128)(2,1)}, u32[]{:S(2)}, u32[]{:S(2)}) async-start(bf16[128,2,4096]{2,1,0:T(2,128)(2,1)} %reshape.219), calls=%async_computation.1 | async-start | bytes 4194304 | tf_op jit(solution)/shard_map/all_to_all | solution.py:13
  94.2 214.7 %reduce-scatter.2.cloned.1.call-start = ((), (), s32[]{:S(2)}) async-start(), calls=%async_computation.5 | async-start | bytes 21233664 | tf_op jit(solution)/shard_map/reduce_scatter | solution.py:111
  129.5 38.8 %copy-start.5 = (bf16[256,768]{1,0:T(8,128)(2,1)S(1)}, bf16[256,768]{1,0:T(8,128)(2,1)}, u32[]{:S(2)}) copy-start(bf16[256,768]{1,0:T(8,128)(2,1)} %copy-done.4) | copy-start | bytes 1179652
  168.3 3.6 %copy-start.3 = (bf16[256,4096]{1,0:T(8,128)(2,1)S(1)}, bf16[256,4096]{1,0:T(8,128)(2,1)}, u32[]{:S(2)}) copy-start(bf16[256,4096]{1,0:T(8,128)(2,1)} %reshape.220) | copy-start | bytes 6291460
  168.3 3.6 %copy-start.8 = (f32[256,768]{1,0:T(8,128)S(1)}, f32[256,768]{1,0:T(8,128)}, u32[]{:S(2)}) copy-start(f32[256,768]{1,0:T(8,128)} %copy-done.7) | copy-start | bytes 2359300
  168.3 3.6 %copy-start.9 = (f32[256,768]{1,0:T(8,128)S(1)}, f32[256,768]{1,0:T(8,128)}, u32[]{:S(2)}) copy-start(f32[256,768]{1,0:T(8,128)} %get-tuple-element.36) | copy-start | bytes 2359300
  201.4 44.6 %all-to-all-start.3 = ((bf16[128,2,4096]{2,1,0:T(2,128)(2,1)}), bf16[128,2,4096]{2,1,0:T(2,128)(2,1)S(1)}, u32[]{:S(2)}, u32[]{:S(2)}) async-start(bf16[128,2,4096]{2,1,0:T(2,128)(2,1)} %reshape.221), calls=%async_computation.3 | async-start | bytes 4194304 | tf_op jit(solution)/shard_map/all_to_all | solution.py:13
  248.6 64.4 %copy-start.1 = (bf16[160,4096]{1,0:T(8,128)(2,1)S(1)}, bf16[160,4096]{1,0:T(8,128)(2,1)}, u32[]{:S(2)}) copy-start(bf16[160,4096]{1,0:T(8,128)(2,1)} %param.10) | copy-start | bytes 3932164
Sparse Core Ops, SparseCore 0:
  188.7 120.1 reduce-scatter.1
where the time goes:
time: 326 us; the launch traced here: 320 us
  waiting for transfers between devices  85.4 us (26%)
  blocking collectives  76.1 us (23%)
  local copies, waits for them, and re-layouts  48.3 us (15%)
  other arithmetic  46.1 us (14%)
  matrix products  38.5 us (12%)
  between operations  15.3 us (5%)
  starting transfers between devices  10.4 us (3%)
    all_to_all x2, blocking collectives, move_rows(): lax.all_to_all(payload, ('dp', 'expert'), split_axis=0, concat_axis=0, ti...  76.1 us
    reduce_scatter x1, waiting for transfers between devices, on_device(): lax.psum_scatter(partial_value.astype(jnp.bfloat16), 'dp', scatter_dimens...  47.6 us
    all_to_all x2, waiting for transfers between devices, move_rows(): lax.all_to_all(payload, ('dp', 'expert'), split_axis=0, concat_axis=0, ti...  37.8 us
    all_to_all x2, starting transfers between devices, move_rows(): lax.all_to_all(payload, ('dp', 'expert'), split_axis=0, concat_axis=0, ti...  10.3 us
    scatter-add x1, other arithmetic, on_device(): jnp.zeros((tok_dev, model_width), jnp.float32).at[token_idx]  9.73 us
    scatter-add x1, other arithmetic, on_device(): d_tokens = jnp.zeros((tok_dev, model_width), jnp.float32).at[token_idx].a...  9.7 us
    another operation x1, other arithmetic, backward_rows(): return (pick_dx, jnp.stack([part_g, part_u, part_d]))  8.06 us
  transfers between devices with their start and end apart: 3, of which 3 were waited for; matrix products, arithmetic and copies ran while one was open for 19% of the time, Pallas kernels for 0%

commit v1 on v0

v1 whole, which is shorter than its diff:
```python
import functools

import jax
import jax.numpy as jnp
from jax import lax
from jax.experimental import pallas as pl
from jax.experimental.pallas import tpu as pltpu
from jax.sharding import PartitionSpec as P

MESH = pl.DeviceIdType.MESH
BF = jnp.bfloat16
F32 = jnp.float32
CAP = 2


def dot_nn(a, b):
    return jnp.dot(a, b, preferred_element_type=F32)


def dot_nt(a, b):
    return lax.dot_general(a, b, (((1,), (1,)), ((), ())), preferred_element_type=F32)


def dot_tn(a, b):
    return lax.dot_general(a, b, (((0,), (0,)), ((), ())), preferred_element_type=F32)


def iota(shape, dim):
    return lax.broadcasted_iota(jnp.int32, shape, dim).astype(F32)


def moe_kernel(
    n_dp, n_e,
    count_ref, ids_c, ids_r, rep_c, rep_r, prob_c, prob_r, place_r, place_c,
    tokens, d_out, w_gate, w_up, w_down,
    layer_out, d_tokens, d_gates, g_gate, g_up, g_down,
    sel, pick0, pick1, wcol,
    wg, wu, wd,
    a_send, x_recv, b_send, c_recv, o_recv, d_recv,
    xs, cs, hs, gs, us,
    acc_g, acc_u, acc_h, own_part, part_send, part_recv,
    w_sem, yz_send, yz_recv, fw_send, fw_recv, ag_send, ag_recv, pt_send, pt_recv,
):
    nx = n_dp // 2
    rows = n_dp * CAP
    slots = rows * n_e
    toks, width = tokens.shape
    chunk = width // nx
    half = chunk // 2
    hid = acc_g.shape[1]
    p = lax.axis_index("dp")
    e = lax.axis_index("expert")
    x = p // 2
    core = p % 2

    def at_x(d):
        return {"dp": lax.rem(x + d, nx) * 2 + core}

    sibling = {"dp": x * 2 + 1 - core}

    def cols(j):
        return pl.ds(pl.multiple_of(lax.rem(x + 1 + j, nx) * chunk, chunk), chunk)

    barrier = pltpu.get_barrier_semaphore()

    def greet(d, _):
        pl.semaphore_signal(
            barrier, inc=1, device_id={"expert": lax.rem(e + d, n_e)}, device_id_type=MESH
        )
        return 0

    lax.fori_loop(1, n_e, greet, 0)
    for d in range(1, nx):
        pl.semaphore_signal(barrier, inc=1, device_id=at_x(d), device_id_type=MESH)
    pl.semaphore_signal(barrier, inc=1, device_id=sibling, device_id_type=MESH)

    def load_gate(j):
        return pltpu.make_async_copy(w_gate.at[0, cols(j)], wg.at[j], w_sem.at[0, j])

    def load_up(j):
        return pltpu.make_async_copy(w_up.at[0, cols(j)], wu.at[j], w_sem.at[1, j])

    def load_down(j):
        return pltpu.make_async_copy(w_down.at[0, :, cols(j)], wd.at[j], w_sem.at[2, j])

    for j in range(nx):
        load_gate(j).start()
        load_up(j).start()
    for j in range(nx):
        load_down(j).start()

    count = count_ref[0].astype(F32)
    codes = n_e * n_dp
    tgt_c, tgt_r, dst_c, dst_r, exp_c, exp_r = [], [], [], [], [], []
    for k in range(2):
        ec = ids_c[:, k : k + 1].astype(F32)
        er = ids_r[k : k + 1, :].astype(F32)
        code_c = ec * n_dp + rep_c[:, k : k + 1].astype(F32)
        code_r = er * n_dp + rep_r[k : k + 1, :].astype(F32)
        dc = jnp.sum(
            jnp.where(iota((toks, codes), 1) == code_c, place_r[...].astype(F32), 0.0),
            axis=1, keepdims=True,
        )
        dr = jnp.sum(
            jnp.where(iota((codes, toks), 0) == code_r, place_c[...].astype(F32), 0.0),
            axis=0, keepdims=True,
        )
        exp_c.append(ec)
        exp_r.append(er)
        dst_c.append(dc)
        dst_r.append(dr)
        tgt_c.append(dc * n_e + ec)
        tgt_r.append(dr * n_e + er)
    t_sub = iota((toks, toks), 0)
    t_lane = iota((toks, toks), 1)
    before_c = (t_lane < t_sub) & (t_lane < count)
    before_r = (t_sub < t_lane) & (t_sub < count)
    slot_c, slot_r = [], []
    for k in range(2):
        rank_c = jnp.zeros((toks, 1), F32)
        rank_r = jnp.zeros((1, toks), F32)
        for m in range(2):
            rank_c += jnp.sum(
                jnp.where((tgt_c[k] == tgt_r[m]) & before_c, 1.0, 0.0), axis=1, keepdims=True
            )
            rank_r += jnp.sum(
                jnp.where((tgt_c[m] == tgt_r[k]) & before_r, 1.0, 0.0), axis=0, keepdims=True
            )
        keep_c = (rank_c < CAP) & (iota((toks, 1), 0) < count)
        keep_r = (rank_r < CAP) & (iota((1, toks), 1) < count)
        slot_c.append(jnp.where(keep_c, exp_c[k] * rows + dst_c[k] * CAP + rank_c, -1.0))
        slot_r.append(jnp.where(keep_r, exp_r[k] * rows + dst_r[k] * CAP + rank_r, -1.0))
    slot_sub = iota((slots, toks), 0)
    slot_lane = iota((toks, slots), 1)
    hit0 = slot_sub == slot_r[0]
    hit1 = slot_sub == slot_r[1]
    sel[...] = jnp.where(hit0 | hit1, 1.0, 0.0).astype(BF)
    wcol[...] = jnp.sum(
        jnp.where(hit0, prob_r[0:1, :], 0.0) + jnp.where(hit1, prob_r[1:2, :], 0.0),
        axis=1, keepdims=True,
    )
    pick0[...] = jnp.where(slot_lane == slot_c[0], 1.0, 0.0).astype(BF)
    pick1[...] = jnp.where(slot_lane == slot_c[1], 1.0, 0.0).astype(BF)

    def block(i):
        return pl.ds(pl.multiple_of(i * rows, rows), rows)

    def exchange(stage, src, dst, j):
        def one(d, _):
            q = lax.rem(e + d, n_e)
            pltpu.make_async_remote_copy(
                src.at[j, block(q)], dst.at[j, block(e)],
                yz_send.at[stage, j], yz_recv.at[stage, j],
                device_id={"expert": q}, device_id_type=MESH,
            ).start()
            return 0

        lax.fori_loop(1, n_e, one, 0)
        pltpu.make_async_copy(
            src.at[j, block(e)], dst.at[j, block(e)], yz_recv.at[stage, j]
        ).start()

    def arrived(stage, dst, j):
        pltpu.make_async_copy(dst.at[j], dst.at[j], yz_recv.at[stage, j]).wait()

    def sent(stage, src, j):
        part = src.at[j, pl.ds(0, slots - rows)]
        pltpu.make_async_copy(part, part, yz_send.at[stage, j]).wait()

    def forward(which, src, dst, j):
        return pltpu.make_async_remote_copy(
            src.at[j], dst.at[j], fw_send.at[which, j], fw_recv.at[which, j],
            device_id=at_x(j + 1), device_id_type=MESH,
        )

    def spread(which, buf, d):
        return pltpu.make_async_remote_copy(
            buf.at[0], buf.at[d], ag_send.at[which, d - 1], ag_recv.at[which, d - 1],
            device_id=at_x(d), device_id_type=MESH,
        )

    def gather_x(j):
        a_send[j] = dot_nn(sel[...], tokens[:, cols(j)]).astype(BF)

    gather_x(0)
    pl.semaphore_wait(barrier, n_e - 1 + nx - 1 + 1)
    exchange(0, a_send, x_recv, 0)

    def first(j, _):
        gather_x(j)
        exchange(0, a_send, x_recv, j)
        return 0

    lax.fori_loop(1, nx, first, 0)

    def gather_cot(j, _):
        raw = dot_nn(sel[...], d_out[:, cols(j)])
        b_send[j] = (raw * wcol[...]).astype(BF)
        return 0

    lax.fori_loop(0, nx, gather_cot, 0)

    acc_g[...] = jnp.zeros_like(acc_g)
    acc_u[...] = jnp.zeros_like(acc_u)
    acc_h[...] = jnp.zeros_like(acc_h)

    def pre_step(j, _):
        arrived(0, x_recv, j)
        exchange(1, b_send, c_recv, j)

        @pl.when(j < nx - 1)
        def _():
            forward(0, x_recv, xs, j).start()

        load_gate(j).wait()
        load_up(j).wait()
        acc_g[...] += dot_nn(x_recv[j], wg[j])
        acc_u[...] += dot_nn(x_recv[j], wu[j])
        return 0

    lax.fori_loop(0, nx, pre_step, 0)

    band = min(32, slots)

    def activate(i, _):
        r = pl.ds(pl.multiple_of(i * band, band), band)
        pre_g = acc_g[r, :]
        pre_u = acc_u[r, :]
        sig = jax.nn.sigmoid(pre_g)
        val = pre_g * sig
        hs[0, r, :] = (val * pre_u).astype(BF)
        acc_g[r, :] = pre_u * (sig * (1.0 + pre_g * (1.0 - sig)))
        acc_u[r, :] = val
        return 0

    lax.fori_loop(0, slots // band, activate, 0)
    for d in range(1, nx):
        spread(0, hs, d).start()

    def cot_step(j, _):
        arrived(1, c_recv, j)

        @pl.when(j < nx - 1)
        def _():
            forward(1, c_recv, cs, j).start()

        load_down(j).wait()
        sent(0, a_send, j)
        a_send[j] = dot_nn(hs[0], wd[j]).astype(BF)
        exchange(2, a_send, o_recv, j)
        acc_h[...] += dot_nt(c_recv[j], wd[j])
        return 0

    lax.fori_loop(0, nx, cot_step, 0)

    def slopes(i, _):
        r = pl.ds(pl.multiple_of(i * band, band), band)
        d_h = acc_h[r, :]
        gs[0, r, :] = (d_h * acc_g[r, :]).astype(BF)
        us[0, r, :] = (d_h * acc_u[r, :]).astype(BF)
        return 0

    lax.fori_loop(0, slots // band, slopes, 0)
    for d in range(1, nx):
        spread(1, gs, d).start()
    for d in range(1, nx):
        spread(2, us, d).start()

    def dx_step(j, _):
        sent(1, b_send, j)
        b_send[j] = (dot_nt(gs[0], wg[j]) + dot_nt(us[0], wu[j])).astype(BF)
        exchange(3, b_send, d_recv, j)
        return 0

    lax.fori_loop(0, nx, dx_step, 0)

    def out_step(j, carry):
        g0, g1 = carry
        arrived(2, o_recv, j)
        got = o_recv[j]
        out0 = dot_nn(pick0[...], got)
        out1 = dot_nn(pick1[...], got)
        cot = d_out[:, cols(j)].astype(F32)
        layer_out[:, cols(j)] = (prob_c[:, 0:1] * out0 + prob_c[:, 1:2] * out1).astype(BF)
        g0 = g0 + jnp.sum(cot * out0, axis=1, keepdims=True)
        g1 = g1 + jnp.sum(cot * out1, axis=1, keepdims=True)
        return g0, g1

    zero = jnp.zeros((toks, 1), F32)
    g0, g1 = lax.fori_loop(0, nx, out_step, (zero, zero))
    d_gates[...] = jnp.where(lax.broadcasted_iota(jnp.int32, (toks, 2), 1) == 0, g0, g1)

    tile = half // 2 if half % 256 == 0 else half

    def row_block(which, d):
        if which == 0:
            return x_recv.at[nx - 1] if d == 0 else xs.at[d - 1]
        return c_recv.at[nx - 1] if d == 0 else cs.at[d - 1]

    def grad_tile(which, start):
        c = pl.ds(pl.multiple_of(start, tile), tile)
        total = None
        for d in range(nx):
            if which == 2:
                term = dot_tn(hs[d], row_block(1, d)[:, c])
            else:
                term = dot_tn(row_block(0, d)[:, c], (gs if which == 0 else us)[d])
            total = term if total is None else total + term
        return total

    def part_copy(which):
        return pltpu.make_async_remote_copy(
            part_send.at[which], part_recv.at[which], pt_send.at[which], pt_recv.at[which],
            device_id=sibling, device_id_type=MESH,
        )

    def put(ref, which, t, value):
        if which == 2:
            ref[t] = value
        else:
            ref[which, pl.ds(t * tile, tile), :] = value

    def grads(which):
        for d in range(1, nx):
            if which == 2:
                forward(1, c_recv, cs, d - 1).wait_recv()
                spread(0, hs, d).wait_recv()
            elif which == 0:
                forward(0, x_recv, xs, d - 1).wait_recv()
                spread(1, gs, d).wait_recv()
            else:
                spread(2, us, d).wait_recv()

    down_send, down_own, down_recv = part_send[1], own_part[1], part_recv[1]
    part_send, own_part, part_recv = part_send[0], own_part[0], part_recv[0]

    def down_copy():
        return pltpu.make_async_remote_copy(
            down_send, down_recv, pt_send.at[2], pt_recv.at[2],
            device_id=sibling, device_id_type=MESH,
        )

    grads(2)
    for t in range(half // tile):
        down_send[:, pl.ds(t * tile, tile)] = grad_tile(2, (1 - core) * half + t * tile).astype(BF)
    down_copy().start()
    for t in range(half // tile):
        down_own[:, pl.ds(t * tile, tile)] = grad_tile(2, core * half + t * tile)
    for which in (0, 1):
        grads(which)
        for t in range(half // tile):
            part_send[which, pl.ds(t * tile, tile), :] = grad_tile(
                which, (1 - core) * half + t * tile
            ).astype(BF)
        part_copy(which).start()
        for t in range(half // tile):
            own_part[which, pl.ds(t * tile, tile), :] = grad_tile(which, core * half + t * tile)

    def tok_step(j, _):
        arrived(3, d_recv, j)
        both = pick0[...] + pick1[...]
        d_tokens[:, cols(j)] = dot_nn(both, d_recv[j]).astype(BF)
        return 0

    lax.fori_loop(0, nx, tok_step, 0)

    down_copy().wait_recv()
    g_down[0] = (down_own[...] + down_recv[...].astype(F32)).astype(BF)
    part_copy(0).wait_recv()
    g_gate[0] = (own_part[0] + part_recv[0].astype(F32)).astype(BF)
    part_copy(1).wait_recv()
    g_up[0] = (own_part[1] + part_recv[1].astype(F32)).astype(BF)

    down_copy().wait_send()
    for which in (0, 1):
        part_copy(which).wait_send()

    def drain(j, _):
        sent(2, a_send, j)
        sent(3, b_send, j)
        return 0

    lax.fori_loop(0, nx, drain, 0)
    for d in range(1, nx):
        forward(0, x_recv, xs, d - 1).wait_send()
        forward(1, c_recv, cs, d - 1).wait_send()
        spread(0, hs, d).wait_send()
        spread(1, gs, d).wait_send()
        spread(2, us, d).wait_send()


def on_device(
    tokens, gate_probs, expert_ids, placement, replica, row_counts, w_gate, w_up, w_down, d_out
):
    n_dp = lax.axis_size("dp")
    n_e = lax.axis_size("expert")
    nx = n_dp // 2
    toks, width = tokens.shape
    hid = w_gate.shape[2]
    slots = n_dp * CAP * n_e
    chunk = width // nx
    half = chunk // 2
    vmem = pl.BlockSpec(memory_space=pltpu.VMEM)
    hbm = pl.BlockSpec(memory_space=pl.ANY)
    smem = pl.BlockSpec(memory_space=pltpu.SMEM)
    yz = (nx, slots, chunk)
    near = (nx - 1, slots, chunk)
    wide = (nx, slots, hid)
    dma = pltpu.SemaphoreType.DMA
    flops = 18 * slots * width * hid
    return pl.pallas_call(
        functools.partial(moe_kernel_entry, n_dp, n_e),
        out_shape=(
            jax.ShapeDtypeStruct((toks, width), BF),
            jax.ShapeDtypeStruct((toks, width), BF),
            jax.ShapeDtypeStruct((toks, 2), F32),
            jax.ShapeDtypeStruct((1, half, hid), BF),
            jax.ShapeDtypeStruct((1, half, hid), BF),
            jax.ShapeDtypeStruct((1, hid, half), BF),
        ),
        in_specs=[smem] + [vmem] * 10 + [hbm] * 3,
        out_specs=[vmem] * 6,
        scratch_shapes=[
            pltpu.VMEM((slots, toks), BF),
            pltpu.VMEM((toks, slots), BF),
            pltpu.VMEM((toks, slots), BF),
            pltpu.VMEM((slots, 1), F32),
            pltpu.VMEM((nx, chunk, hid), BF),
            pltpu.VMEM((nx, chunk, hid), BF),
            pltpu.VMEM((nx, hid, chunk), BF),
            pltpu.VMEM(yz, BF),
            pltpu.VMEM(yz, BF),
            pltpu.VMEM(yz, BF),
            pltpu.VMEM(yz, BF),
            pltpu.VMEM(yz, BF),
            pltpu.VMEM(yz, BF),
            pltpu.VMEM(near, BF),
            pltpu.VMEM(near, BF),
            pltpu.VMEM(wide, BF),
            pltpu.VMEM(wide, BF),
            pltpu.VMEM(wide, BF),
            pltpu.VMEM((slots, hid), F32),
            pltpu.VMEM((slots, hid), F32),
            pltpu.VMEM((slots, hid), F32),
            pltpu.VMEM((2, half, hid), F32),
            pltpu.VMEM((hid, half), F32),
            pltpu.VMEM((2, half, hid), BF),
            pltpu.VMEM((hid, half), BF),
            pltpu.VMEM((2, half, hid), BF),
            pltpu.VMEM((hid, half), BF),
            dma((3, nx)),
            dma((4, nx)),
            dma((4, nx)),
            dma((2, nx - 1)),
            dma((2, nx - 1)),
            dma((3, nx - 1)),
            dma((3, nx - 1)),
            dma((3,)),
            dma((3,)),
        ],
        compiler_params=pltpu.CompilerParams(
            collective_id=0, has_side_effects=True, vmem_limit_bytes=62 << 20
        ),
        cost_estimate=pl.CostEstimate(flops=flops, bytes_accessed=6 * width * hid, transcendentals=0),
        name="moe",
    )(
        row_counts, expert_ids, expert_ids.T, replica, replica.T, gate_probs, gate_probs.T,
        placement.reshape(1, n_e * n_dp), placement.reshape(n_e * n_dp, 1),
        tokens, d_out, w_gate, w_up, w_down,
    )


def moe_kernel_entry(n_dp, n_e, *refs):
    head, rest = refs[:41], refs[41:]
    own_part, down_own, part_send, down_send, part_recv, down_recv = rest[:6]
    moe_kernel(
        n_dp, n_e, *head,
        (own_part, down_own), (part_send, down_send), (part_recv, down_recv), *rest[6:],
    )


def solution(mesh):
    rows = P(("dp", "expert"), None)
    weight = P("expert", None, None)
    return jax.shard_map(
        on_device,
        mesh=mesh,
        in_specs=(
            rows, rows, rows, P(), rows, P(("dp", "expert")), weight, weight, weight, rows,
        ),
        out_specs=(
            rows, rows, rows,
            P("expert", "dp", None), P("expert", "dp", None), P("expert", None, "dp"),
        ),
        check_vma=False,
    )
```

time: 326 us -> 145 us (0.44)
  the two profiles are of different devices: /device:TPU:1 before, /device:TPU:31 now
where the time goes in v1:
time: 145 us
  Pallas kernels  128 us (88%)
  local copies, waits for them, and re-layouts  15.3 us (11%)
    pallas_call x1, Pallas kernels, on_device(): pl.pallas_call(functools.partial(moe_kernel_entry, n_dp, n_e), out_shape=...  128 us
    unnamed x17, local copies, waits for them, and re-layouts  12.4 us

profile of v1, /device:TPU:31, one launch (start us, length us, event | category | flops | bytes accessed | tf_op | source)
XLA Modules:
  0.0 144.7 jit_solution(13418515210810522011)
XLA Ops:
  1.3 0.8 copy.23
  2.0 0.6 reshape.18.refs_7_
  2.6 0.7 reshape.20.refs_8_
  3.4 1.4 copy.27.refs_5_
  4.8 1.4 copy.25.refs_1_
  6.2 1.4 copy.26.refs_3_
  7.6 128.1 %moe.1 = (bf16[160,4096]{1,0:T(8,128)(2,1)}, bf16[160,4096]{1,0:T(8,128)(2,1)}, f32[160,2]{1,0:T(8,128)}, bf16[1,512,768]{2,1,0:T(8,128)(2,1)}, bf16[1,512,768]{...) custom-call(s32[1]{0:T(128)S(6)} %copy.35.refs_0_, s32[160,2]{1,0:T(8,128)} %copy.25.refs_1_, s32[2,160]{1,0:T(2,128)} %bitcast.3, ...), custom_call_target="tpu_custom_call" | custom-call | flops 14495514624 | bytes 18874368 | tf_op jit(solution)/shard_map/moe/pallas_call | solution.py:411
  135.8 1.5 %copy.29 = f32[160,2]{0,1:T(2,128)} copy(f32[160,2]{1,0:T(8,128)} %get-tuple-element.14) | data formatting | bytes 2560 | tf_op jit(solution)/shard_map/moe/pallas_call | solution.py:411
  137.3 0.0 copy-start
  137.3 2.6 %copy.36 = bf16[160,4096]{1,0:T(8,128)(2,1)} copy(bf16[160,4096]{1,0:T(8,128)(2,1)} %get-tuple-element.24) | data formatting | bytes 2621440
  139.9 0.0 copy-done
  139.9 0.0 copy-start.3
  139.9 1.1 copy.37
  141.0 0.5 copy-done.3
  141.5 0.0 copy-start.2
  141.5 0.0 copy-start.1
  141.5 0.9 copy.38
  142.4 0.5 copy-done.2
  143.0 0.9 copy.39
  143.8 0.0 copy-done.1
  143.8 0.9 copy.40
Async XLA Ops:
  137.3 2.6 %copy-start = (bf16[160,4096]{1,0:T(8,128)(2,1)S(1)}, bf16[160,4096]{1,0:T(8,128)(2,1)}, u32[]{:S(2)}) copy-start(bf16[160,4096]{1,0:T(8,128)(2,1)} %get-tuple-element.25) | copy-start | bytes 3932164
  139.9 1.6 %copy-start.3 = (bf16[1,512,768]{2,1,0:T(8,128)(2,1)S(1)}, bf16[1,512,768]{2,1,0:T(8,128)(2,1)}, u32[]{:S(2)}) copy-start(bf16[1,512,768]{2,1,0:T(8,128)(2,1)} %get-tuple-element.27) | copy-start | bytes 2359300
  141.5 1.4 copy-start.2
  141.5 2.3 %copy-start.1 = (bf16[1,768,512]{2,1,0:T(8,128)(2,1)S(1)}, bf16[1,768,512]{2,1,0:T(8,128)(2,1)}, u32[]{:S(2)}) copy-start(bf16[1,768,512]{2,1,0:T(8,128)(2,1)} %get-tuple-element.29) | copy-start | bytes 2359300

commit v2 on v1

v2 whole, which is shorter than its diff:
```python
import functools

import jax
import jax.numpy as jnp
from jax import lax
from jax.experimental import pallas as pl
from jax.experimental.pallas import tpu as pltpu
from jax.sharding import PartitionSpec as P

MESH = pl.DeviceIdType.MESH
BF = jnp.bfloat16
F32 = jnp.float32
CAP = 2


def dot_nn(a, b):
    return jnp.dot(a, b, preferred_element_type=F32)


def dot_nt(a, b):
    return lax.dot_general(a, b, (((1,), (1,)), ((), ())), preferred_element_type=F32)


def dot_tn(a, b):
    return lax.dot_general(a, b, (((0,), (0,)), ((), ())), preferred_element_type=F32)


def iota(shape, dim):
    return lax.broadcasted_iota(jnp.int32, shape, dim).astype(F32)


def moe_kernel(
    n_dp, n_e,
    count_ref, ids_r, rep_r, prob_r, place_t,
    tokens_hbm, d_out_hbm, w_gate, w_up, w_down,
    layer_out, d_tokens, d_gates, g_gate, g_up, g_down,
    tokens, d_out, lo_buf, dt_buf,
    sel, pick0, pick1, wcol, prob_c,
    wg, wu, wd,
    a_send, x_recv, b_send, c_recv, o_recv, d_recv,
    xs, cs, hs, gs, us,
    acc_g, acc_u, acc_h,
    gu_own, down_own, gu_send, down_send, gu_recv, down_recv, gu_out, down_out,
    w_sem, t_sem, out_sem,
    yz_send, yz_recv, fw_send, fw_recv, ag_send, ag_recv, pt_send, pt_recv,
):
    nx = n_dp // 2
    rows = n_dp * CAP
    slots = rows * n_e
    toks, width = tokens_hbm.shape
    chunk = width // nx
    half = chunk // 2
    p = lax.axis_index("dp")
    e = lax.axis_index("expert")
    x = p // 2
    core = p % 2

    def at_x(d):
        return {"dp": lax.rem(x + d, nx) * 2 + core}

    sibling = {"dp": x * 2 + 1 - core}

    def cols(j):
        return pl.ds(pl.multiple_of(lax.rem(x + 1 + j, nx) * chunk, chunk), chunk)

    barrier = pltpu.get_barrier_semaphore()

    def greet(d, _):
        pl.semaphore_signal(
            barrier, inc=1, device_id={"expert": lax.rem(e + d, n_e)}, device_id_type=MESH
        )
        return 0

    lax.fori_loop(1, n_e, greet, 0)
    for d in range(1, nx):
        pl.semaphore_signal(barrier, inc=1, device_id=at_x(d), device_id_type=MESH)
    pl.semaphore_signal(barrier, inc=1, device_id=sibling, device_id_type=MESH)

    def load_gate(j):
        return pltpu.make_async_copy(w_gate.at[0, cols(j)], wg.at[j], w_sem.at[0, j])

    def load_up(j):
        return pltpu.make_async_copy(w_up.at[0, cols(j)], wu.at[j], w_sem.at[1, j])

    def load_down(j):
        return pltpu.make_async_copy(w_down.at[0, :, cols(j)], wd.at[j], w_sem.at[2, j])

    def load_tok(j):
        return pltpu.make_async_copy(tokens_hbm.at[:, cols(j)], tokens.at[j], t_sem.at[0, j])

    def load_cot(j):
        return pltpu.make_async_copy(d_out_hbm.at[:, cols(j)], d_out.at[j], t_sem.at[1, j])

    for j in range(nx):
        load_tok(j).start()
    for j in range(nx):
        load_cot(j).start()
        load_gate(j).start()
        load_up(j).start()
    for j in range(nx):
        load_down(j).start()

    count = count_ref[0].astype(F32)
    place = place_t[...].astype(F32).astype(BF)
    tgt_r, dst_r, exp_r = [], [], []
    for k in range(2):
        er = ids_r[k : k + 1, :].astype(F32)
        rr = rep_r[k : k + 1, :].astype(F32)
        of_expert = jnp.where(iota((n_e, toks), 0) == er, 1.0, 0.0).astype(BF)
        holders = dot_nn(place, of_expert)
        dr = jnp.sum(jnp.where(iota((n_dp, toks), 0) == rr, holders, 0.0), axis=0, keepdims=True)
        exp_r.append(er)
        dst_r.append(dr)
        tgt_r.append(dr * n_e + er)
    t_sub = iota((toks, toks), 0)
    t_lane = iota((toks, toks), 1)
    diagonal = t_sub == t_lane

    def as_column(row):
        return jnp.sum(jnp.where(diagonal, row, 0.0), axis=1, keepdims=True)

    tgt_c = [as_column(tgt_r[k]) for k in range(2)]
    before = (t_sub < t_lane) & (t_sub < count)
    slot_r = []
    for k in range(2):
        rank = jnp.zeros((1, toks), F32)
        for m in range(2):
            rank += jnp.sum(
                jnp.where((tgt_c[m] == tgt_r[k]) & before, 1.0, 0.0), axis=0, keepdims=True
            )
        keep = (rank < CAP) & (iota((1, toks), 1) < count)
        slot_r.append(jnp.where(keep, exp_r[k] * rows + dst_r[k] * CAP + rank, -1.0))
    slot_sub = iota((slots, toks), 0)
    slot_lane = iota((toks, slots), 1)
    hit0 = slot_sub == slot_r[0]
    hit1 = slot_sub == slot_r[1]
    sel[...] = jnp.where(hit0 | hit1, 1.0, 0.0).astype(BF)
    wcol[...] = jnp.sum(
        jnp.where(hit0, prob_r[0:1, :], 0.0) + jnp.where(hit1, prob_r[1:2, :], 0.0),
        axis=1, keepdims=True,
    )

    def rest_of_routing():
        pick0[...] = jnp.where(slot_lane == as_column(slot_r[0]), 1.0, 0.0).astype(BF)
        pick1[...] = jnp.where(slot_lane == as_column(slot_r[1]), 1.0, 0.0).astype(BF)
        prob_c[0] = as_column(prob_r[0:1, :])
        prob_c[1] = as_column(prob_r[1:2, :])

    def block(i):
        return pl.ds(pl.multiple_of(i * rows, rows), rows)

    def exchange(stage, src, dst, j):
        def one(d, _):
            q = lax.rem(e + d, n_e)
            pltpu.make_async_remote_copy(
                src.at[j, block(q)], dst.at[j, block(e)],
                yz_send.at[stage, j], yz_recv.at[stage, j],
                device_id={"expert": q}, device_id_type=MESH,
            ).start()
            return 0

        lax.fori_loop(1, n_e, one, 0)
        pltpu.make_async_copy(
            src.at[j, block(e)], dst.at[j, block(e)], yz_recv.at[stage, j]
        ).start()

    def arrived(stage, dst, j):
        pltpu.make_async_copy(dst.at[j], dst.at[j], yz_recv.at[stage, j]).wait()

    def sent(stage, src, j):
        part = src.at[j, pl.ds(0, slots - rows)]
        pltpu.make_async_copy(part, part, yz_send.at[stage, j]).wait()

    def forward(which, src, dst, j):
        return pltpu.make_async_remote_copy(
            src.at[j], dst.at[j], fw_send.at[which, j], fw_recv.at[which, j],
            device_id=at_x(j + 1), device_id_type=MESH,
        )

    cut = slots // 2

    def hand(which, buf, way):
        return pltpu.make_async_remote_copy(
            buf.at[0], buf.at[1 if way == 0 else nx - 1],
            ag_send.at[which, way], ag_recv.at[which, way],
            device_id=at_x(1 if way == 0 else nx - 1), device_id_type=MESH,
        )

    def relay(which, buf, way):
        r = pl.ds(way * cut, cut)
        return pltpu.make_async_remote_copy(
            buf.at[1 if way == 0 else nx - 1, r], buf.at[2, r],
            ag_send.at[which, 2 + way], ag_recv.at[which, 2 + way],
            device_id=at_x(1 if way == 0 else nx - 1), device_id_type=MESH,
        )

    def hand_out(which, buf):
        for way in (0, 1):
            hand(which, buf, way).start()

    def pass_on(which, buf):
        for way in (0, 1):
            hand(which, buf, way).wait_recv()
            relay(which, buf, way).start()

    def all_here(which, buf):
        for way in (0, 1):
            relay(which, buf, way).wait_recv()

    def gather_x(j):
        load_tok(j).wait()
        a_send[j] = dot_nn(sel[...], tokens[j]).astype(BF)

    gather_x(0)
    pl.semaphore_wait(barrier, n_e - 1 + nx - 1 + 1)
    exchange(0, a_send, x_recv, 0)

    def first(j, _):
        gather_x(j)
        exchange(0, a_send, x_recv, j)
        return 0

    lax.fori_loop(1, nx, first, 0)
    rest_of_routing()

    def gather_cot(j, _):
        load_cot(j).wait()
        raw = dot_nn(sel[...], d_out[j])
        b_send[j] = (raw * wcol[...]).astype(BF)
        return 0

    lax.fori_loop(0, nx, gather_cot, 0)

    acc_g[...] = jnp.zeros_like(acc_g)
    acc_u[...] = jnp.zeros_like(acc_u)
    acc_h[...] = jnp.zeros_like(acc_h)

    def pre_step(j, _):
        arrived(0, x_recv, j)
        exchange(1, b_send, c_recv, j)

        @pl.when(j < nx - 1)
        def _():
            forward(0, x_recv, xs, j).start()

        load_gate(j).wait()
        load_up(j).wait()
        acc_g[...] += dot_nn(x_recv[j], wg[j])
        acc_u[...] += dot_nn(x_recv[j], wu[j])
        return 0

    lax.fori_loop(0, nx, pre_step, 0)

    band = min(32, slots)

    def activate(i, _):
        r = pl.ds(pl.multiple_of(i * band, band), band)
        pre_g = acc_g[r, :]
        pre_u = acc_u[r, :]
        sig = jax.nn.sigmoid(pre_g)
        val = pre_g * sig
        hs[0, r, :] = (val * pre_u).astype(BF)
        acc_g[r, :] = pre_u * (sig * (1.0 + pre_g * (1.0 - sig)))
        acc_u[r, :] = val
        return 0

    lax.fori_loop(0, slots // band, activate, 0)
    hand_out(0, hs)

    def cot_step(j, _):
        @pl.when(j == nx - 1)
        def _():
            pass_on(0, hs)

        arrived(1, c_recv, j)

        @pl.when(j < nx - 1)
        def _():
            forward(1, c_recv, cs, j).start()

        load_down(j).wait()
        sent(0, a_send, j)
        a_send[j] = dot_nn(hs[0], wd[j]).astype(BF)
        exchange(2, a_send, o_recv, j)
        acc_h[...] += dot_nt(c_recv[j], wd[j])
        return 0

    lax.fori_loop(0, nx, cot_step, 0)

    def slopes(i, _):
        r = pl.ds(pl.multiple_of(i * band, band), band)
        d_h = acc_h[r, :]
        gs[0, r, :] = (d_h * acc_g[r, :]).astype(BF)
        us[0, r, :] = (d_h * acc_u[r, :]).astype(BF)
        return 0

    lax.fori_loop(0, slots // band, slopes, 0)
    hand_out(1, gs)
    hand_out(2, us)

    def dx_step(j, _):
        sent(1, b_send, j)
        b_send[j] = (dot_nt(gs[0], wg[j]) + dot_nt(us[0], wu[j])).astype(BF)
        exchange(3, b_send, d_recv, j)
        return 0

    lax.fori_loop(0, nx, dx_step, 0)

    def out_copy(j):
        return pltpu.make_async_copy(lo_buf.at[j], layer_out.at[:, cols(j)], out_sem.at[0, j])

    def tok_copy(j):
        return pltpu.make_async_copy(dt_buf.at[j], d_tokens.at[:, cols(j)], out_sem.at[1, j])

    def out_step(j, carry):
        g0, g1 = carry

        @pl.when(j == nx - 2)
        def _():
            pass_on(1, gs)

        @pl.when(j == nx - 1)
        def _():
            pass_on(2, us)

        arrived(2, o_recv, j)
        got = o_recv[j]
        out0 = dot_nn(pick0[...], got)
        out1 = dot_nn(pick1[...], got)
        cot = d_out[j].astype(F32)
        lo_buf[j] = (prob_c[0] * out0 + prob_c[1] * out1).astype(BF)
        out_copy(j).start()
        g0 = g0 + jnp.sum(cot * out0, axis=1, keepdims=True)
        g1 = g1 + jnp.sum(cot * out1, axis=1, keepdims=True)
        return g0, g1

    zero = jnp.zeros((toks, 1), F32)
    g0, g1 = lax.fori_loop(0, nx, out_step, (zero, zero))

    def as_row(column):
        return jnp.sum(jnp.where(diagonal, column, 0.0), axis=0, keepdims=True)

    d_gates[0:1, :] = as_row(g0)
    d_gates[1:2, :] = as_row(g1)

    tile = half // 2 if half % 256 == 0 else half

    def row_block(which, d):
        if which == 0:
            return x_recv.at[nx - 1] if d == 0 else xs.at[d - 1]
        return c_recv.at[nx - 1] if d == 0 else cs.at[d - 1]

    def grad_tile(which, start):
        c = pl.ds(pl.multiple_of(start, tile), tile)
        total = None
        for d in range(nx):
            if which == 2:
                term = dot_tn(hs[d], row_block(1, d)[:, c])
            else:
                term = dot_tn(row_block(0, d)[:, c], (gs if which == 0 else us)[d])
            total = term if total is None else total + term
        return total

    def part_copy(which):
        src, dst = (gu_send.at[which], gu_recv.at[which]) if which < 2 else (down_send, down_recv)
        return pltpu.make_async_remote_copy(
            src, dst, pt_send.at[which], pt_recv.at[which],
            device_id=sibling, device_id_type=MESH,
        )

    def grad_copy(which):
        if which == 2:
            return pltpu.make_async_copy(down_out, g_down.at[0], out_sem.at[2, 2])
        return pltpu.make_async_copy(
            gu_out.at[which], (g_gate, g_up)[which].at[0], out_sem.at[2, which]
        )

    def grads(which):
        if which == 2:
            for d in range(1, nx):
                forward(1, c_recv, cs, d - 1).wait_recv()
            all_here(0, hs)
        elif which == 0:
            for d in range(1, nx):
                forward(0, x_recv, xs, d - 1).wait_recv()
            all_here(1, gs)
        else:
            all_here(2, us)
        for t in range(half // tile):
            value = grad_tile(which, (1 - core) * half + t * tile).astype(BF)
            if which == 2:
                down_send[:, pl.ds(t * tile, tile)] = value
            else:
                gu_send[which, pl.ds(t * tile, tile), :] = value
        part_copy(which).start()
        for t in range(half // tile):
            value = grad_tile(which, core * half + t * tile)
            if which == 2:
                down_own[:, pl.ds(t * tile, tile)] = value
            else:
                gu_own[which, pl.ds(t * tile, tile), :] = value

    def finish(which):
        part_copy(which).wait_recv()
        if which == 2:
            down_out[...] = (down_own[...] + down_recv[...].astype(F32)).astype(BF)
        else:
            gu_out[which] = (gu_own[which] + gu_recv[which].astype(F32)).astype(BF)
        grad_copy(which).start()

    def tok_step(j):
        arrived(3, d_recv, j)
        dt_buf[j] = dot_nn(pick0[...] + pick1[...], d_recv[j]).astype(BF)
        tok_copy(j).start()

    grads(2)
    finish(2)
    tok_step(0)
    grads(0)
    tok_step(1)
    grads(1)
    finish(0)
    tok_step(2)
    finish(1)
    tok_step(3)

    for which in range(3):
        part_copy(which).wait_send()
        grad_copy(which).wait()

    def drain(j, _):
        sent(2, a_send, j)
        sent(3, b_send, j)
        out_copy(j).wait()
        tok_copy(j).wait()
        return 0

    lax.fori_loop(0, nx, drain, 0)
    for d in range(1, nx):
        forward(0, x_recv, xs, d - 1).wait_send()
        forward(1, c_recv, cs, d - 1).wait_send()
    for which, buf in enumerate((hs, gs, us)):
        for way in (0, 1):
            hand(which, buf, way).wait_send()
            relay(which, buf, way).wait_send()


def place_kernel(*refs):
    n = (len(refs) - 1) // 3
    src, dst, hold, sems = refs[:n], refs[n : 2 * n], refs[2 * n : 3 * n], refs[-1]
    loads, stores = [], []
    for i in range(n):
        dim = len(src[i].shape) - 2
        pieces = 2 if src[i].shape[dim] >= 32 else 1
        size = src[i].shape[dim] // pieces
        for piece in range(pieces):
            at = (slice(None),) * dim + (pl.ds(piece * size, size),)
            loads.append(pltpu.make_async_copy(src[i].at[at], hold[i].at[at], sems.at[0, i, piece]))
            stores.append(pltpu.make_async_copy(hold[i].at[at], dst[i].at[at], sems.at[1, i, piece]))
    for copy in loads:
        copy.start()
    for load, store in zip(loads, stores):
        load.wait()
        store.start()
    for copy in stores:
        copy.wait()


def on_device(
    tokens, gate_probs, expert_ids, placement, replica, row_counts, w_gate, w_up, w_down, d_out
):
    n_dp = lax.axis_size("dp")
    n_e = lax.axis_size("expert")
    nx = n_dp // 2
    toks, width = tokens.shape
    hid = w_gate.shape[2]
    slots = n_dp * CAP * n_e
    chunk = width // nx
    half = chunk // 2
    vmem = pl.BlockSpec(memory_space=pltpu.VMEM)
    hbm = pl.BlockSpec(memory_space=pl.ANY)
    smem = pl.BlockSpec(memory_space=pltpu.SMEM)
    yz = (nx, slots, chunk)
    near = (nx - 1, slots, chunk)
    wide = (nx, slots, hid)
    dma = pltpu.SemaphoreType.DMA
    flops = 18 * slots * width * hid
    outs = (
        jax.ShapeDtypeStruct((toks, width), BF),
        jax.ShapeDtypeStruct((toks, width), BF),
        jax.ShapeDtypeStruct((2, toks), F32),
        jax.ShapeDtypeStruct((1, half, hid), BF),
        jax.ShapeDtypeStruct((1, half, hid), BF),
        jax.ShapeDtypeStruct((1, hid, half), BF),
    )
    mine = (nx, toks, chunk)
    results = pl.pallas_call(
        functools.partial(moe_kernel, n_dp, n_e),
        out_shape=outs,
        in_specs=[smem] + [vmem] * 4 + [hbm] * 5,
        out_specs=[hbm, hbm, vmem, hbm, hbm, hbm],
        scratch_shapes=[
            pltpu.VMEM(mine, BF),
            pltpu.VMEM(mine, BF),
            pltpu.VMEM(mine, BF),
            pltpu.VMEM(mine, BF),
            pltpu.VMEM((slots, toks), BF),
            pltpu.VMEM((toks, slots), BF),
            pltpu.VMEM((toks, slots), BF),
            pltpu.VMEM((slots, 1), F32),
            pltpu.VMEM((2, toks, 1), F32),
            pltpu.VMEM((nx, chunk, hid), BF),
            pltpu.VMEM((nx, chunk, hid), BF),
            pltpu.VMEM((nx, hid, chunk), BF),
            pltpu.VMEM(yz, BF),
            pltpu.VMEM(yz, BF),
            pltpu.VMEM(yz, BF),
            pltpu.VMEM(yz, BF),
            pltpu.VMEM(yz, BF),
            pltpu.VMEM(yz, BF),
            pltpu.VMEM(near, BF),
            pltpu.VMEM(near, BF),
            pltpu.VMEM(wide, BF),
            pltpu.VMEM(wide, BF),
            pltpu.VMEM(wide, BF),
            pltpu.VMEM((slots, hid), F32),
            pltpu.VMEM((slots, hid), F32),
            pltpu.VMEM((slots, hid), F32),
            pltpu.VMEM((2, half, hid), F32),
            pltpu.VMEM((hid, half), F32),
            pltpu.VMEM((2, half, hid), BF),
            pltpu.VMEM((hid, half), BF),
            pltpu.VMEM((2, half, hid), BF),
            pltpu.VMEM((hid, half), BF),
            pltpu.VMEM((2, half, hid), BF),
            pltpu.VMEM((hid, half), BF),
            dma((3, nx)),
            dma((2, nx)),
            dma((3, nx)),
            dma((4, nx)),
            dma((4, nx)),
            dma((2, nx - 1)),
            dma((2, nx - 1)),
            dma((3, 4)),
            dma((3, 4)),
            dma((3,)),
            dma((3,)),
        ],
        compiler_params=pltpu.CompilerParams(
            collective_id=0, has_side_effects=True, vmem_limit_bytes=62 << 20
        ),
        cost_estimate=pl.CostEstimate(flops=flops, bytes_accessed=6 * width * hid, transcendentals=0),
        name="moe",
    )(
        row_counts, expert_ids.T, replica.T, gate_probs.T, placement.T,
        tokens, d_out, w_gate, w_up, w_down,
    )
    results = pl.pallas_call(
        place_kernel,
        out_shape=outs,
        in_specs=[hbm] * 6,
        out_specs=[hbm] * 6,
        scratch_shapes=[pltpu.VMEM(out.shape, out.dtype) for out in outs] + [dma((2, 6, 2))],
        name="place",
    )(*results)
    layer_out, d_tokens, d_gates, g_gate, g_up, g_down = results
    return layer_out, d_tokens, d_gates.T, g_gate, g_up, g_down


def solution(mesh):
    rows = P(("dp", "expert"), None)
    weight = P("expert", None, None)
    return jax.shard_map(
        on_device,
        mesh=mesh,
        in_specs=(
            rows, rows, rows, P(), rows, P(("dp", "expert")), weight, weight, weight, rows,
        ),
        out_specs=(
            rows, rows, rows,
            P("expert", "dp", None), P("expert", "dp", None), P("expert", None, "dp"),
        ),
        check_vma=False,
    )
```

time: 145 us -> 122 us (0.84)
  local copies, waits for them, and re-layouts: 15.3 us -> 0 us
  Pallas kernels: 128 us -> 120 us
    unnamed x17 -> x0, local copies, waits for them, and re-layouts: 12.4 us -> none
    pallas_call x1 -> x2, Pallas kernels: 128 us -> 120 us  [the longest x1 116 us: on_device(): pl.pallas_call(functools.partial(moe_kernel, n_dp, n_e), out_shape=outs,...]
    pallas_call x1 -> x0, local copies, waits for them, and re-layouts: 1.54 us -> none  [on_device(): pl.pallas_call(functools.partial(moe_kernel_entry, n_dp, n_e), out_shape=...]
where the time goes in v2:
time: 122 us; the launch traced here: 121 us
  Pallas kernels  120 us (98%)
  between operations  1.29 us (1%)
    pallas_call x1, Pallas kernels, on_device(): pl.pallas_call(functools.partial(moe_kernel, n_dp, n_e), out_shape=outs,...  116 us
    pallas_call x1, Pallas kernels, on_device(): pl.pallas_call(place_kernel, out_shape=outs, in_specs=[hbm] * 6, out_spec...  4.33 us

profile of v2, /device:TPU:31, one launch (start us, length us, event | category | flops | bytes accessed | tf_op | source)
XLA Modules:
  0.0 121.2 jit_solution(952223113106995834)
XLA Ops:
  1.3 115.6 %moe.1 = (bf16[160,4096]{1,0:T(8,128)(2,1)}, bf16[160,4096]{1,0:T(8,128)(2,1)}, f32[2,160]{1,0:T(2,128)}, bf16[1,512,768]{2,1,0:T(8,128)(2,1)}, bf16[1,512,768]{...) custom-call(s32[1]{0:T(128)S(6)} %copy.16.count_ref, s32[2,160]{1,0:T(2,128)} %bitcast.6, s32[2,160]{1,0:T(2,128)} %bitcast.7, ...), custom_call_target="tpu_custom_call" | custom-call | flops 14495514624 | bytes 18874368 | tf_op jit(solution)/shard_map/moe/pallas_call | solution.py:497
  116.9 4.3 %place.1 = (bf16[160,4096]{1,0:T(8,128)(2,1)}, bf16[160,4096]{1,0:T(8,128)(2,1)}, f32[2,160]{1,0:T(2,128)}, bf16[1,512,768]{2,1,0:T(8,128)(2,1)}, bf16[1,512,768...) custom-call(bf16[160,4096]{1,0:T(8,128)(2,1)} %get-tuple-element.18.refs_0_, bf16[160,4096]{1,0:T(8,128)(2,1)} %get-tuple-element.19.refs_1_, ...), custom_call_target="tpu_custom_call" | custom-call | tf_op jit(solution)/shard_map/place/pallas_call | solution.py:558

commit v3 on v2

--- a/solution.py
+++ b/solution.py
@@ -34,15 +34,15 @@
     count_ref, ids_r, rep_r, prob_r, place_t,
     tokens_hbm, d_out_hbm, w_gate, w_up, w_down,
     layer_out, d_tokens, d_gates, g_gate, g_up, g_down,
-    tokens, d_out, lo_buf, dt_buf,
+    tokens, d_out,
     sel, pick0, pick1, wcol, prob_c,
     wg, wu, wd,
     a_send, x_recv, b_send, c_recv, o_recv, d_recv,
-    xs, cs, hs, gs, us,
-    acc_g, acc_u, acc_h,
-    gu_own, down_own, gu_send, down_send, gu_recv, down_recv, gu_out, down_out,
-    w_sem, t_sem, out_sem,
+    xs, cot_sib, hs, h_sib, gs, us, r_send, r_mid, r_end,
+    acc, gu_acc, gu_send, gu_recv,
+    w_sem, t_sem,
     yz_send, yz_recv, fw_send, fw_recv, ag_send, ag_recv, pt_send, pt_recv,
+    sib_send, sib_recv, ring_send, ring_recv,
 ):
     nx = n_dp // 2
     rows = n_dp * CAP
@@ -50,6 +50,8 @@
     toks, width = tokens_hbm.shape
     chunk = width // nx
     half = chunk // 2
+    acc_g, acc_u, acc_h = (acc.at[pl.ds(i * slots, slots)] for i in range(3))
+    hid = w_down.shape[1]
     p = lax.axis_index("dp")
     e = lax.axis_index("expert")
     x = p // 2
@@ -60,8 +62,15 @@
 
     sibling = {"dp": x * 2 + 1 - core}
 
+    order = (2, 1, 3, 0)
+
+    def away(j):
+        if isinstance(j, int):
+            return order[j]
+        return jnp.where(j == 0, 2, jnp.where(j == 1, 1, jnp.where(j == 2, 3, 0)))
+
     def cols(j):
-        return pl.ds(pl.multiple_of(lax.rem(x + 1 + j, nx) * chunk, chunk), chunk)
+        return pl.ds(pl.multiple_of(lax.rem(x + away(j), nx) * chunk, chunk), chunk)
 
     barrier = pltpu.get_barrier_semaphore()
 
@@ -171,11 +180,46 @@
         part = src.at[j, pl.ds(0, slots - rows)]
         pltpu.make_async_copy(part, part, yz_send.at[stage, j]).wait()
 
-    def forward(which, src, dst, j):
-        return pltpu.make_async_remote_copy(
-            src.at[j], dst.at[j], fw_send.at[which, j], fw_recv.at[which, j],
-            device_id=at_x(j + 1), device_id_type=MESH,
-        )
+    def forward(j):
+        return pltpu.make_async_remote_copy(
+            x_recv.at[j], xs.at[j], fw_send.at[j], fw_recv.at[j],
+            device_id=at_x(away(j)), device_id_type=MESH,
+        )
+
+    other = pl.multiple_of((1 - core) * half, half)
+    mine = pl.multiple_of(core * half, half)
+
+    def hidden_over():
+        return pltpu.make_async_remote_copy(
+            hs, h_sib, sib_send.at[nx], sib_recv.at[nx],
+            device_id=sibling, device_id_type=MESH,
+        )
+
+    def cot_over(j):
+        return pltpu.make_async_remote_copy(
+            c_recv.at[j, :, pl.ds(other, half)], cot_sib.at[j], sib_send.at[j], sib_recv.at[j],
+            device_id=sibling, device_id_type=MESH,
+        )
+
+    rcut = hid // 2
+
+    def ring_half(way):
+        r = pl.ds(way * rcut, rcut)
+        return pltpu.make_async_remote_copy(
+            r_send.at[0, r], r_mid.at[way], ring_send.at[way], ring_recv.at[way],
+            device_id=at_x(1 if way == 0 else nx - 1), device_id_type=MESH,
+        )
+
+    def ring_whole(way):
+        return pltpu.make_async_remote_copy(
+            r_send.at[1 + way], r_end.at[way], ring_send.at[2 + way], ring_recv.at[2 + way],
+            device_id=at_x(1 if way == 0 else nx - 1), device_id_type=MESH,
+        )
+
+    def down_part(j, start, size):
+        c = pl.ds(start, size)
+        m = pl.ds(pl.multiple_of(mine + start, size), size)
+        return dot_tn(hs[...], c_recv[j, :, m]) + dot_tn(h_sib[...], cot_sib[j, :, c])
 
     cut = slots // 2
 
@@ -217,7 +261,11 @@
 
     def first(j, _):
         gather_x(j)
-        exchange(0, a_send, x_recv, j)
+
+        @pl.when(j < 2)
+        def _():
+            exchange(0, a_send, x_recv, j)
+
         return 0
 
     lax.fori_loop(1, nx, first, 0)
@@ -237,11 +285,24 @@
 
     def pre_step(j, _):
         arrived(0, x_recv, j)
-        exchange(1, b_send, c_recv, j)
+
+        @pl.when(j == 0)
+        def _():
+            for later in range(2, nx):
+                exchange(0, a_send, x_recv, later)
+
+        @pl.when(j > 0)
+        def _():
+            exchange(1, b_send, c_recv, j - 1)
+
+        @pl.when(j == nx - 1)
+        def _():
+            exchange(1, b_send, c_recv, j)
+
 
         @pl.when(j < nx - 1)
         def _():
-            forward(0, x_recv, xs, j).start()
+            forward(j).start()
 
         load_gate(j).wait()
         load_up(j).wait()
@@ -259,33 +320,47 @@
         pre_u = acc_u[r, :]
         sig = jax.nn.sigmoid(pre_g)
         val = pre_g * sig
-        hs[0, r, :] = (val * pre_u).astype(BF)
+        hs[r, :] = (val * pre_u).astype(BF)
         acc_g[r, :] = pre_u * (sig * (1.0 + pre_g * (1.0 - sig)))
         acc_u[r, :] = val
         return 0
 
     lax.fori_loop(0, slots // band, activate, 0)
-    hand_out(0, hs)
+    hidden_over().start()
+
+    tile = half // 2
+    tiles = [(t * tile, pl.ds(t * tile, tile)) for t in range(half // tile)]
 
     def cot_step(j, _):
-        @pl.when(j == nx - 1)
-        def _():
-            pass_on(0, hs)
-
         arrived(1, c_recv, j)
-
-        @pl.when(j < nx - 1)
-        def _():
-            forward(1, c_recv, cs, j).start()
-
+        cot_over(j).start()
         load_down(j).wait()
         sent(0, a_send, j)
-        a_send[j] = dot_nn(hs[0], wd[j]).astype(BF)
+        a_send[j] = dot_nn(hs[...], wd[j]).astype(BF)
         exchange(2, a_send, o_recv, j)
         acc_h[...] += dot_nt(c_recv[j], wd[j])
         return 0
 
-    lax.fori_loop(0, nx, cot_step, 0)
+    cot_step(0, 0)
+    hidden_over().wait_recv()
+    cot_over(0).wait_recv()
+    for start, r in tiles:
+        r_send[0, :, r] = down_part(0, start, tile).astype(BF)
+    for way in (0, 1):
+        ring_half(way).start()
+    for way in (0, 1):
+        cot_step(1 + way, 0)
+        cot_over(1 + way).wait_recv()
+        ring_half(way).wait_recv()
+        part = pl.ds(way * rcut, rcut)
+        rest = pl.ds((1 - way) * rcut, rcut)
+        for start, r in tiles:
+            value = down_part(1 + way, start, tile)
+            with_mid = value[way * rcut : (way + 1) * rcut] + r_mid[way, :, r].astype(F32)
+            r_send[1 + way, part, r] = with_mid.astype(BF)
+            r_send[1 + way, rest, r] = value[(1 - way) * rcut : (2 - way) * rcut].astype(BF)
+        ring_whole(way).start()
+    cot_step(nx - 1, 0)
 
     def slopes(i, _):
         r = pl.ds(pl.multiple_of(i * band, band), band)
@@ -295,8 +370,8 @@
         return 0
 
     lax.fori_loop(0, slots // band, slopes, 0)
-    hand_out(1, gs)
-    hand_out(2, us)
+    hand_out(0, gs)
+    hand_out(1, us)
 
     def dx_step(j, _):
         sent(1, b_send, j)
@@ -306,36 +381,24 @@
 
     lax.fori_loop(0, nx, dx_step, 0)
 
-    def out_copy(j):
-        return pltpu.make_async_copy(lo_buf.at[j], layer_out.at[:, cols(j)], out_sem.at[0, j])
-
-    def tok_copy(j):
-        return pltpu.make_async_copy(dt_buf.at[j], d_tokens.at[:, cols(j)], out_sem.at[1, j])
-
     def out_step(j, carry):
         g0, g1 = carry
-
-        @pl.when(j == nx - 2)
-        def _():
-            pass_on(1, gs)
-
-        @pl.when(j == nx - 1)
-        def _():
-            pass_on(2, us)
-
         arrived(2, o_recv, j)
         got = o_recv[j]
         out0 = dot_nn(pick0[...], got)
         out1 = dot_nn(pick1[...], got)
         cot = d_out[j].astype(F32)
-        lo_buf[j] = (prob_c[0] * out0 + prob_c[1] * out1).astype(BF)
-        out_copy(j).start()
+        layer_out[:, cols(j)] = (prob_c[0] * out0 + prob_c[1] * out1).astype(BF)
         g0 = g0 + jnp.sum(cot * out0, axis=1, keepdims=True)
         g1 = g1 + jnp.sum(cot * out1, axis=1, keepdims=True)
         return g0, g1
 
     zero = jnp.zeros((toks, 1), F32)
-    g0, g1 = lax.fori_loop(0, nx, out_step, (zero, zero))
+    carry = lax.fori_loop(0, nx - 2, out_step, (zero, zero))
+    pass_on(0, gs)
+    carry = out_step(nx - 2, carry)
+    pass_on(1, us)
+    g0, g1 = out_step(nx - 1, carry)
 
     def as_row(column):
         return jnp.sum(jnp.where(diagonal, column, 0.0), axis=0, keepdims=True)
@@ -343,126 +406,103 @@
     d_gates[0:1, :] = as_row(g0)
     d_gates[1:2, :] = as_row(g1)
 
-    tile = half // 2 if half % 256 == 0 else half
-
-    def row_block(which, d):
-        if which == 0:
-            return x_recv.at[nx - 1] if d == 0 else xs.at[d - 1]
-        return c_recv.at[nx - 1] if d == 0 else cs.at[d - 1]
-
-    def grad_tile(which, start):
+    def row_block(d):
+        if d == 0:
+            return x_recv.at[nx - 1]
+        return xs.at[order.index(d)]
+
+    def grad_tile(which, start, blocks):
         c = pl.ds(pl.multiple_of(start, tile), tile)
         total = None
-        for d in range(nx):
-            if which == 2:
-                term = dot_tn(hs[d], row_block(1, d)[:, c])
-            else:
-                term = dot_tn(row_block(0, d)[:, c], (gs if which == 0 else us)[d])
+        for d in blocks:
+            term = dot_tn(row_block(d)[:, c], (gs, us)[which][d])
             total = term if total is None else total + term
         return total
 
     def part_copy(which):
-        src, dst = (gu_send.at[which], gu_recv.at[which]) if which < 2 else (down_send, down_recv)
-        return pltpu.make_async_remote_copy(
-            src, dst, pt_send.at[which], pt_recv.at[which],
+        return pltpu.make_async_remote_copy(
+            gu_send.at[which], gu_recv.at[which], pt_send.at[which], pt_recv.at[which],
             device_id=sibling, device_id_type=MESH,
         )
 
-    def grad_copy(which):
-        if which == 2:
-            return pltpu.make_async_copy(down_out, g_down.at[0], out_sem.at[2, 2])
-        return pltpu.make_async_copy(
-            gu_out.at[which], (g_gate, g_up)[which].at[0], out_sem.at[2, which]
-        )
-
-    def grads(which):
-        if which == 2:
-            for d in range(1, nx):
-                forward(1, c_recv, cs, d - 1).wait_recv()
-            all_here(0, hs)
-        elif which == 0:
-            for d in range(1, nx):
-                forward(0, x_recv, xs, d - 1).wait_recv()
-            all_here(1, gs)
-        else:
-            all_here(2, us)
-        for t in range(half // tile):
-            value = grad_tile(which, (1 - core) * half + t * tile).astype(BF)
-            if which == 2:
-                down_send[:, pl.ds(t * tile, tile)] = value
-            else:
-                gu_send[which, pl.ds(t * tile, tile), :] = value
+    near_blocks = [0, 1, nx - 1]
+
+    def first_blocks(which):
+        for start, r in tiles:
+            gu_acc[which, 0, r, :] = grad_tile(which, other + start, near_blocks)
+            gu_acc[which, 1, r, :] = grad_tile(which, mine + start, near_blocks)
+
+    def last_block(which):
+        all_here(which, (gs, us)[which])
+        for start, r in tiles:
+            last = grad_tile(which, other + start, [2])
+            gu_send[which, r, :] = (gu_acc[which, 0, r, :] + last).astype(BF)
         part_copy(which).start()
-        for t in range(half // tile):
-            value = grad_tile(which, core * half + t * tile)
-            if which == 2:
-                down_own[:, pl.ds(t * tile, tile)] = value
-            else:
-                gu_own[which, pl.ds(t * tile, tile), :] = value
+        for start, r in tiles:
+            gu_acc[which, 1, r, :] += grad_tile(which, mine + start, [2])
 
     def finish(which):
         part_copy(which).wait_recv()
-        if which == 2:
-            down_out[...] = (down_own[...] + down_recv[...].astype(F32)).astype(BF)
-        else:
-            gu_out[which] = (gu_own[which] + gu_recv[which].astype(F32)).astype(BF)
-        grad_copy(which).start()
+        (g_gate, g_up)[which][0] = (
+            gu_acc[which, 1] + gu_recv[which].astype(F32)
+        ).astype(BF)
+
+    def finish_down():
+        for way in (0, 1):
+            ring_whole(way).wait_recv()
+        cot_over(nx - 1).wait_recv()
+        for start, r in tiles:
+            value = down_part(nx - 1, start, tile)
+            value += r_end[0, :, r].astype(F32) + r_end[1, :, r].astype(F32)
+            g_down[0, :, r] = value.astype(BF)
 
     def tok_step(j):
         arrived(3, d_recv, j)
-        dt_buf[j] = dot_nn(pick0[...] + pick1[...], d_recv[j]).astype(BF)
-        tok_copy(j).start()
-
-    grads(2)
-    finish(2)
+        d_tokens[:, cols(j)] = dot_nn(pick0[...] + pick1[...], d_recv[j]).astype(BF)
+
+    for j in range(nx - 1):
+        forward(j).wait_recv()
+    first_blocks(0)
+    first_blocks(1)
+    finish_down()
     tok_step(0)
-    grads(0)
+    last_block(0)
     tok_step(1)
-    grads(1)
+    last_block(1)
     finish(0)
     tok_step(2)
     finish(1)
     tok_step(3)
 
-    for which in range(3):
+    for which in (0, 1):
         part_copy(which).wait_send()
-        grad_copy(which).wait()
 
     def drain(j, _):
         sent(2, a_send, j)
         sent(3, b_send, j)
-        out_copy(j).wait()
-        tok_copy(j).wait()
         return 0
 
     lax.fori_loop(0, nx, drain, 0)
-    for d in range(1, nx):
-        forward(0, x_recv, xs, d - 1).wait_send()
-        forward(1, c_recv, cs, d - 1).wait_send()
-    for which, buf in enumerate((hs, gs, us)):
+    for j in range(nx - 1):
+        forward(j).wait_send()
+    for j in range(nx):
+        cot_over(j).wait_send()
+    hidden_over().wait_send()
+    for way in (0, 1):
+        ring_half(way).wait_send()
+        ring_whole(way).wait_send()
+    for which, buf in enumerate((gs, us)):
         for way in (0, 1):
             hand(which, buf, way).wait_send()
             relay(which, buf, way).wait_send()
 
 
 def place_kernel(*refs):
-    n = (len(refs) - 1) // 3
-    src, dst, hold, sems = refs[:n], refs[n : 2 * n], refs[2 * n : 3 * n], refs[-1]
-    loads, stores = [], []
-    for i in range(n):
-        dim = len(src[i].shape) - 2
-        pieces = 2 if src[i].shape[dim] >= 32 else 1
-        size = src[i].shape[dim] // pieces
-        for piece in range(pieces):
-            at = (slice(None),) * dim + (pl.ds(piece * size, size),)
-            loads.append(pltpu.make_async_copy(src[i].at[at], hold[i].at[at], sems.at[0, i, piece]))
-            stores.append(pltpu.make_async_copy(hold[i].at[at], dst[i].at[at], sems.at[1, i, piece]))
-    for copy in loads:
+    n = (len(refs) - 1) // 2
+    copies = [pltpu.make_async_copy(refs[i], refs[n + i], refs[-1].at[i]) for i in range(n)]
+    for copy in copies:
         copy.start()
-    for load, store in zip(loads, stores):
-        load.wait()
-        store.start()
-    for copy in stores:
+    for copy in copies:
         copy.wait()
 
 
@@ -496,12 +536,10 @@
     mine = (nx, toks, chunk)
     results = pl.pallas_call(
         functools.partial(moe_kernel, n_dp, n_e),
-        out_shape=outs,
+        out_shape=[pltpu.VMEM(out.shape, out.dtype) for out in outs],
         in_specs=[smem] + [vmem] * 4 + [hbm] * 5,
-        out_specs=[hbm, hbm, vmem, hbm, hbm, hbm],
+        out_specs=[vmem] * 6,
         scratch_shapes=[
-            pltpu.VMEM(mine, BF),
-            pltpu.VMEM(mine, BF),
             pltpu.VMEM(mine, BF),
             pltpu.VMEM(mine, BF),
             pltpu.VMEM((slots, toks), BF),
@@ -519,35 +557,35 @@
             pltpu.VMEM(yz, BF),
             pltpu.VMEM(yz, BF),
             pltpu.VMEM(near, BF),
-            pltpu.VMEM(near, BF),
+            pltpu.VMEM((nx, slots, half), BF),
+            pltpu.VMEM((slots, hid), BF),
+            pltpu.VMEM((slots, hid), BF),
             pltpu.VMEM(wide, BF),
             pltpu.VMEM(wide, BF),
-            pltpu.VMEM(wide, BF),
-            pltpu.VMEM((slots, hid), F32),
-            pltpu.VMEM((slots, hid), F32),
-            pltpu.VMEM((slots, hid), F32),
-            pltpu.VMEM((2, half, hid), F32),
-            pltpu.VMEM((hid, half), F32),
+            pltpu.VMEM((3, hid, half), BF),
+            pltpu.VMEM((2, hid // 2, half), BF),
+            pltpu.VMEM((2, hid, half), BF),
+            pltpu.VMEM((3 * slots, hid), F32),
+            pltpu.VMEM((2, 2, half, hid), F32),
             pltpu.VMEM((2, half, hid), BF),
-            pltpu.VMEM((hid, half), BF),
             pltpu.VMEM((2, half, hid), BF),
-            pltpu.VMEM((hid, half), BF),
-            pltpu.VMEM((2, half, hid), BF),
-            pltpu.VMEM((hid, half), BF),
             dma((3, nx)),
             dma((2, nx)),
-            dma((3, nx)),
             dma((4, nx)),
             dma((4, nx)),
-            dma((2, nx - 1)),
-            dma((2, nx - 1)),
-            dma((3, 4)),
-            dma((3, 4)),
-            dma((3,)),
-            dma((3,)),
+            dma((nx - 1,)),
+            dma((nx - 1,)),
+            dma((2, 4)),
+            dma((2, 4)),
+            dma((2,)),
+            dma((2,)),
+            dma((nx + 1,)),
+            dma((nx + 1,)),
+            dma((4,)),
+            dma((4,)),
         ],
         compiler_params=pltpu.CompilerParams(
-            collective_id=0, has_side_effects=True, vmem_limit_bytes=62 << 20
+            collective_id=0, has_side_effects=True, vmem_limit_bytes=58 << 20
         ),
         cost_estimate=pl.CostEstimate(flops=flops, bytes_accessed=6 * width * hid, transcendentals=0),
         name="moe",
@@ -560,9 +598,10 @@
         out_shape=outs,
         in_specs=[hbm] * 6,
         out_specs=[hbm] * 6,
-        scratch_shapes=[pltpu.VMEM(out.shape, out.dtype) for out in outs] + [dma((2, 6, 2))],
+        scratch_shapes=[dma((6,))],
+        compiler_params=pltpu.CompilerParams(vmem_limit_bytes=1 << 20),
         name="place",
-    )(*results)
+    )(*[pltpu.with_memory_space_constraint(result, pltpu.VMEM) for result in results])
     layer_out, d_tokens, d_gates, g_gate, g_up, g_down = results
     return layer_out, d_tokens, d_gates.T, g_gate, g_up, g_down
 

time: 122 us -> 111 us (0.910)
  Pallas kernels: 120 us -> 109 us
    pallas_call x1, Pallas kernels: 116 us -> 107 us  [on_device(): pl.pallas_call(functools.partial(moe_kernel, n_dp, n_e), out_shape=[pltpu...]
    pallas_call x1, Pallas kernels: 4.33 us -> 2.32 us  [on_device(): pl.pallas_call(place_kernel, out_shape=outs, in_specs=[hbm] * 6, out_spec...]
where the time goes in v3:
time: 111 us
  Pallas kernels  109 us (98%)
  between operations  1.45 us (1%)
    pallas_call x1, Pallas kernels, on_device(): pl.pallas_call(functools.partial(moe_kernel, n_dp, n_e), out_shape=[pltpu...  107 us
    pallas_call x1, Pallas kernels, on_device(): pl.pallas_call(place_kernel, out_shape=outs, in_specs=[hbm] * 6, out_spec...  2.32 us

profile of v3, /device:TPU:31, one launch (start us, length us, event | category | flops | bytes accessed | tf_op | source)
XLA Modules:
  0.0 110.6 jit_solution(11272377468952861100)
XLA Ops:
  1.3 106.8 %moe.1 = (bf16[160,4096]{1,0:T(8,128)(2,1)S(1)}, bf16[160,4096]{1,0:T(8,128)(2,1)S(1)}, f32[2,160]{1,0:T(2,128)S(1)}, bf16[1,512,768]{2,1,0:T(8,128)(2,1)S(1)}, ...) custom-call(s32[1]{0:T(128)S(6)} %copy.16.count_ref, s32[2,160]{1,0:T(2,128)} %bitcast.6, ...), custom_call_target="tpu_custom_call" | custom-call | flops 14495514624 | bytes 18874368 | tf_op jit(solution)/shard_map/moe/pallas_call | solution.py:537
  108.1 2.3 %place.1 = (bf16[160,4096]{1,0:T(8,128)(2,1)}, bf16[160,4096]{1,0:T(8,128)(2,1)}, f32[2,160]{1,0:T(2,128)}, bf16[1,512,768]{2,1,0:T(8,128)(2,1)}, bf16[1,512,768...) custom-call(bf16[160,4096]{1,0:T(8,128)(2,1)S(1)} %get-tuple-element.18.refs_0_, ...), custom_call_target="tpu_custom_call" | custom-call | tf_op jit(solution)/shard_map/place/pallas_call | solution.py:596

commit v4 on v3

--- a/solution.py
+++ b/solution.py
@@ -31,16 +31,17 @@
 
 def moe_kernel(
     n_dp, n_e,
-    count_ref, ids_r, rep_r, prob_r, place_t,
+    count_hbm, ids_hbm, rep_hbm, prob_hbm, place_hbm,
     tokens_hbm, d_out_hbm, w_gate, w_up, w_down,
     layer_out, d_tokens, d_gates, g_gate, g_up, g_down,
+    count_ref, ids_r, rep_r, prob_r, place_t,
     tokens, d_out,
     sel, pick0, pick1, wcol, prob_c,
     wg, wu, wd,
     a_send, x_recv, b_send, c_recv, o_recv, d_recv,
     xs, cot_sib, hs, h_sib, gs, us, r_send, r_mid, r_end,
     acc, gu_acc, gu_send, gu_recv,
-    w_sem, t_sem,
+    s_sem, w_sem, t_sem,
     yz_send, yz_recv, fw_send, fw_recv, ag_send, ag_recv, pt_send, pt_recv,
     sib_send, sib_recv, ring_send, ring_recv,
 ):
@@ -72,6 +73,16 @@
     def cols(j):
         return pl.ds(pl.multiple_of(lax.rem(x + away(j), nx) * chunk, chunk), chunk)
 
+    small = [
+        pltpu.make_async_copy(src, dst, s_sem.at[i])
+        for i, (src, dst) in enumerate((
+            (ids_hbm, ids_r), (rep_hbm, rep_r), (place_hbm, place_t),
+            (count_hbm, count_ref), (prob_hbm, prob_r),
+        ))
+    ]
+    for copy in small:
+        copy.start()
+
     barrier = pltpu.get_barrier_semaphore()
 
     def greet(d, _):
@@ -109,6 +120,8 @@
     for j in range(nx):
         load_down(j).start()
 
+    for copy in small:
+        copy.wait()
     count = count_ref[0].astype(F32)
     place = place_t[...].astype(F32).astype(BF)
     tgt_r, dst_r, exp_r = [], [], []
@@ -144,23 +157,25 @@
     hit0 = slot_sub == slot_r[0]
     hit1 = slot_sub == slot_r[1]
     sel[...] = jnp.where(hit0 | hit1, 1.0, 0.0).astype(BF)
-    wcol[...] = jnp.sum(
-        jnp.where(hit0, prob_r[0:1, :], 0.0) + jnp.where(hit1, prob_r[1:2, :], 0.0),
-        axis=1, keepdims=True,
-    )
 
     def rest_of_routing():
+        wcol[...] = jnp.sum(
+            jnp.where(hit0, prob_r[0:1, :], 0.0) + jnp.where(hit1, prob_r[1:2, :], 0.0),
+            axis=1, keepdims=True,
+        )
         pick0[...] = jnp.where(slot_lane == as_column(slot_r[0]), 1.0, 0.0).astype(BF)
         pick1[...] = jnp.where(slot_lane == as_column(slot_r[1]), 1.0, 0.0).astype(BF)
         prob_c[0] = as_column(prob_r[0:1, :])
         prob_c[1] = as_column(prob_r[1:2, :])
 
+    side = 4
+
     def block(i):
         return pl.ds(pl.multiple_of(i * rows, rows), rows)
 
     def exchange(stage, src, dst, j):
         def one(d, _):
-            q = lax.rem(e + d, n_e)
+            q = lax.rem(e // side + d // side, side) * side + lax.rem(e % side + d % side, side)
             pltpu.make_async_remote_copy(
                 src.at[j, block(q)], dst.at[j, block(e)],
                 yz_send.at[stage, j], yz_recv.at[stage, j],
@@ -348,8 +363,9 @@
         r_send[0, :, r] = down_part(0, start, tile).astype(BF)
     for way in (0, 1):
         ring_half(way).start()
+    cot_step(1, 0)
+    cot_step(2, 0)
     for way in (0, 1):
-        cot_step(1 + way, 0)
         cot_over(1 + way).wait_recv()
         ring_half(way).wait_recv()
         part = pl.ds(way * rcut, rcut)
@@ -519,7 +535,6 @@
     half = chunk // 2
     vmem = pl.BlockSpec(memory_space=pltpu.VMEM)
     hbm = pl.BlockSpec(memory_space=pl.ANY)
-    smem = pl.BlockSpec(memory_space=pltpu.SMEM)
     yz = (nx, slots, chunk)
     near = (nx - 1, slots, chunk)
     wide = (nx, slots, hid)
@@ -537,9 +552,14 @@
     results = pl.pallas_call(
         functools.partial(moe_kernel, n_dp, n_e),
         out_shape=[pltpu.VMEM(out.shape, out.dtype) for out in outs],
-        in_specs=[smem] + [vmem] * 4 + [hbm] * 5,
+        in_specs=[hbm] * 10,
         out_specs=[vmem] * 6,
         scratch_shapes=[
+            pltpu.SMEM((1,), jnp.int32),
+            pltpu.VMEM((2, toks), jnp.int32),
+            pltpu.VMEM((2, toks), jnp.int32),
+            pltpu.VMEM((2, toks), F32),
+            pltpu.VMEM((n_dp, n_e), jnp.int32),
             pltpu.VMEM(mine, BF),
             pltpu.VMEM(mine, BF),
             pltpu.VMEM((slots, toks), BF),
@@ -569,6 +589,7 @@
             pltpu.VMEM((2, 2, half, hid), F32),
             pltpu.VMEM((2, half, hid), BF),
             pltpu.VMEM((2, half, hid), BF),
+            dma((5,)),
             dma((3, nx)),
             dma((2, nx)),
             dma((4, nx)),

time: 111 us -> 107 us (0.964)
  Pallas kernels: 109 us -> 106 us
    pallas_call x1, Pallas kernels: 107 us -> 103 us  [on_device(): pl.pallas_call(functools.partial(moe_kernel, n_dp, n_e), out_shape=[pltpu...]
where the time goes in v4:
time: 107 us
  Pallas kernels  106 us (99%)
  between operations  1.45 us (1%)
    pallas_call x1, Pallas kernels, on_device(): pl.pallas_call(functools.partial(moe_kernel, n_dp, n_e), out_shape=[pltpu...  103 us
    pallas_call x1, Pallas kernels, on_device(): pl.pallas_call(place_kernel, out_shape=outs, in_specs=[hbm] * 6, out_spec...  2.32 us

profile of v4, /device:TPU:31, one launch (start us, length us, event | category | flops | bytes accessed | tf_op | source)
XLA Modules:
  0.0 107.1 jit_solution(14723114513639668088)
XLA Ops:
  1.3 103.3 %moe.1 = (bf16[160,4096]{1,0:T(8,128)(2,1)S(1)}, bf16[160,4096]{1,0:T(8,128)(2,1)S(1)}, f32[2,160]{1,0:T(2,128)S(1)}, bf16[1,512,768]{2,1,0:T(8,128)(2,1)S(1)}, ...) custom-call(s32[1]{0:T(128)S(6)} %copy.16.count_hbm, s32[2,160]{1,0:T(2,128)} %bitcast.6, ...), custom_call_target="tpu_custom_call" | custom-call | flops 14495514624 | bytes 18874368 | tf_op jit(solution)/shard_map/moe/pallas_call | solution.py:552
  104.6 2.3 %place.1 = (bf16[160,4096]{1,0:T(8,128)(2,1)}, bf16[160,4096]{1,0:T(8,128)(2,1)}, f32[2,160]{1,0:T(2,128)}, bf16[1,512,768]{2,1,0:T(8,128)(2,1)}, bf16[1,512,768...) custom-call(bf16[160,4096]{1,0:T(8,128)(2,1)S(1)} %get-tuple-element.18.refs_0_, ...), custom_call_target="tpu_custom_call" | custom-call | tf_op jit(solution)/shard_map/place/pallas_call | solution.py:617

commit v5 on v4

--- a/solution.py
+++ b/solution.py
@@ -376,7 +376,9 @@
             r_send[1 + way, part, r] = with_mid.astype(BF)
             r_send[1 + way, rest, r] = value[(1 - way) * rcut : (2 - way) * rcut].astype(BF)
         ring_whole(way).start()
-    cot_step(nx - 1, 0)
+    arrived(1, c_recv, nx - 1)
+    load_down(nx - 1).wait()
+    acc_h[...] += dot_nt(c_recv[nx - 1], wd[nx - 1])
 
     def slopes(i, _):
         r = pl.ds(pl.multiple_of(i * band, band), band)
@@ -388,6 +390,10 @@
     lax.fori_loop(0, slots // band, slopes, 0)
     hand_out(0, gs)
     hand_out(1, us)
+    cot_over(nx - 1).start()
+    sent(0, a_send, nx - 1)
+    a_send[nx - 1] = dot_nn(hs[...], wd[nx - 1]).astype(BF)
+    exchange(2, a_send, o_recv, nx - 1)
 
     def dx_step(j, _):
         sent(1, b_send, j)

time: 107 us -> 107 us (level)
  no operation moved by 1% of the time
where the time goes in v5:
time: 107 us
  Pallas kernels  105 us (98%)
  between operations  1.45 us (1%)
    pallas_call x1, Pallas kernels, on_device(): pl.pallas_call(functools.partial(moe_kernel, n_dp, n_e), out_shape=[pltpu...  103 us
    pallas_call x1, Pallas kernels, on_device(): pl.pallas_call(place_kernel, out_shape=outs, in_specs=[hbm] * 6, out_spec...  2.32 us

profile of v5, /device:TPU:31, one launch (start us, length us, event | category | flops | bytes accessed | tf_op | source)
XLA Modules:
  0.0 106.8 jit_solution(3139948699481041604)
XLA Ops:
  1.3 103.0 %moe.1 = (bf16[160,4096]{1,0:T(8,128)(2,1)S(1)}, bf16[160,4096]{1,0:T(8,128)(2,1)S(1)}, f32[2,160]{1,0:T(2,128)S(1)}, bf16[1,512,768]{2,1,0:T(8,128)(2,1)S(1)}, ...) custom-call(s32[1]{0:T(128)S(6)} %copy.16.count_hbm, s32[2,160]{1,0:T(2,128)} %bitcast.6, ...), custom_call_target="tpu_custom_call" | custom-call | flops 14495514624 | bytes 18874368 | tf_op jit(solution)/shard_map/moe/pallas_call | solution.py:558
  104.3 2.3 %place.1 = (bf16[160,4096]{1,0:T(8,128)(2,1)}, bf16[160,4096]{1,0:T(8,128)(2,1)}, f32[2,160]{1,0:T(2,128)}, bf16[1,512,768]{2,1,0:T(8,128)(2,1)}, bf16[1,512,768...) custom-call(bf16[160,4096]{1,0:T(8,128)(2,1)S(1)} %get-tuple-element.18.refs_0_, ...), custom_call_target="tpu_custom_call" | custom-call | tf_op jit(solution)/shard_map/place/pallas_call | solution.py:623
